TPU v7x, 32 devices: a whole 2x2x4 slice. The times are simulated.
32 devices in a mesh: ctx: 16 (over z, y, core), head: 2 (over x).
Axes of the slice: x: 2, y: 2, z: 4, core: 2. Of those that a mesh axis runs over, the one named last changes fastest.
Arguments:
- queries: bfloat16 [4096, 8192], P(('ctx', 'head')), may hold values from -200 to 200
- key_rows: bfloat16 [4096, 1024], P(('ctx', 'head')), may hold values from -6 to 6
- value_rows: bfloat16 [4096, 1024], P(('ctx', 'head')), may hold values from -6 to 6
- span_order: int32 [32], replicated, may hold values from 0 to 31, each once
Outputs:
- attended: bfloat16 [4096, 8192], P(('ctx', 'head'))
Inputs may be any that keep to these rules, and one draw needn't show every extreme that they name: Stored span j holds sequence positions span_order[j] * 128 to span_order[j] * 128 + 127; each number appears once.
All inputs are finite; a program needn't handle non-finite values.
Results may differ from a plain program's by a relative error of at most 0.005.
Values may be sent and summed in bfloat16 or wider, within the bound.
No kernel may reach another device: no remote copies, remote signals or barrier semaphores. Data moves between devices by JAX's collectives and lax.ppermute only.
A program may use at most 256 MiB of HBM per device.

v0:
```python
import functools
import math

import jax
import jax.numpy as jnp
from jax import lax
from jax.experimental import pallas as pl
from jax.experimental.pallas import tpu as pltpu
from jax.sharding import Mesh
from jax.sharding import PartitionSpec as P

HQ = 64
KVH = 8
HD = 128
SPAN = 128
GROUP = HQ // KVH
ROWS = GROUP * SPAN
SCALE = HD**-0.5 * math.log2(math.e)
EXTRA = 16
BLOCK = 8
VMEM = 24 * 2**20
NT = (((1,), (1,)), ((), ()))
GROUP_AXES = ("inner", "head")
AWAY = ((5, 7), (1, 4, 3, 6))
HOME = (2, 0)


def queries_of(q_ref):
    return jnp.concatenate([q_ref[:, g * HD : (g + 1) * HD] for g in range(GROUP)], 0)


def scores(keys, q_ref):
    return lax.dot_general(keys, queries_of(q_ref), NT, preferred_element_type=jnp.float32) * SCALE


def blend(values, weights):
    ones = jnp.ones((EXTRA, values.shape[1]), jnp.bfloat16)
    values = jnp.concatenate([values, ones], 0)
    return jnp.dot(values, weights.astype(jnp.bfloat16), preferred_element_type=jnp.float32)


def causal(s):
    key = lax.broadcasted_iota(jnp.int32, (SPAN, ROWS), 0)
    row = lax.broadcasted_iota(jnp.int32, (SPAN, ROWS), 1) % SPAN
    return jnp.where(key <= row, s, -1e30)


def gather(kv_ref, slots):
    return (
        jnp.concatenate([kv_ref[s, :SPAN] for s in slots], 0),
        jnp.concatenate([kv_ref[s, SPAN:] for s in slots], 1),
    )


def listing(order, wanted):
    n = order.shape[0]
    numbers = jnp.arange(n, dtype=jnp.int32)
    before = jnp.logical_and(order[None, :] < order[:, None], wanted[None, :])
    rank = jnp.sum(before.astype(jnp.int32), axis=1)
    mine = jnp.logical_and(rank[None, :] == numbers[:, None], wanted[None, :])
    return rank, jnp.sum(jnp.where(mine, numbers[None, :], 0), axis=1)


class Table:
    def __init__(self, spans):
        self.first, self.far_first, self.bases = 0, 1, 2
        self.order = 16
        self.near_rank, self.near_list, self.far_rank, self.far_list, self.all_list = (
            16 + spans * (1 + t) for t in range(5)
        )
        self.sequence = 16 + spans * 6


def fetch(at, t_ref, pieces, indices, target_of, sems, optional):
    def copy_of(index):
        return pltpu.make_async_copy(pieces[index], target_of(index), sems.at[index])

    for act in ("start", "wait"):
        for index in indices:
            if index in optional:

                @pl.when(t_ref[at.bases + index] >= 0)
                def _(index=index):
                    getattr(copy_of(index), act)()

            else:
                getattr(copy_of(index), act)()


def attend(t_ref, list_at, rank, q_ref, kv_ref, acc_ref, m_ref):
    def first_block(count):
        others = [t_ref[list_at + rank - t] for t in range(1, count)]
        keys, values = gather(kv_ref, [t_ref[list_at + rank], *others])
        s = scores(keys, q_ref)
        own = causal(s[:SPAN])
        m = jnp.max(own, axis=0, keepdims=True)
        s = jnp.concatenate([own, s[SPAN:]], 0) if count > 1 else own
        m_ref[...] = jnp.broadcast_to(m, m_ref.shape)
        acc_ref[...] = blend(values, jnp.exp2(s - m))

    for count in range(1, BLOCK + 1):

        @pl.when(rank % BLOCK == count - 1)
        def _(count=count):
            first_block(count)

    def block(b, carry):
        keys, values = gather(kv_ref, [t_ref[list_at + b * BLOCK + t] for t in range(BLOCK)])
        acc_ref[...] += blend(values, jnp.exp2(scores(keys, q_ref) - m_ref[:1]))
        return carry

    lax.fori_loop(0, rank // BLOCK, block, 0)


def recheck(at, t_ref, p, q_ref, pieces, acc_ref, run_ref, span_ref, sem):
    @pl.when(jnp.logical_not(jnp.max(acc_ref[HD : HD + 8]) < 1e30))
    def _():
        run_ref[...] = jnp.full_like(run_ref, -1e30)
        acc_ref[...] = jnp.zeros_like(acc_ref)
        for index, piece in enumerate(pieces):
            base = t_ref[at.bases + index]

            def careful(j, carry, piece=piece, base=base):
                other = t_ref[at.order + jnp.maximum(base, 0) + j]

                @pl.when(jnp.logical_and(base >= 0, other <= p))
                def _():
                    copy = pltpu.make_async_copy(piece.at[j], span_ref, sem)
                    copy.start()
                    copy.wait()
                    s = scores(span_ref[:SPAN], q_ref)
                    s = jnp.where(other < p, s, causal(s))
                    old = run_ref[...]
                    new = jnp.maximum(old, jnp.max(s, axis=0, keepdims=True))
                    run_ref[...] = new
                    fresh = blend(span_ref[SPAN:], jnp.exp2(s - new[:1]))
                    acc_ref[...] = acc_ref[...] * jnp.exp2(old - new)[:1] + fresh

                return carry

            lax.fori_loop(0, piece.shape[0], careful, 0)


def conclude(acc_ref, o_ref):
    result = acc_ref[:HD] * (1.0 / acc_ref[HD : HD + 1])
    for g in range(GROUP):
        o_ref[:, g * HD : (g + 1) * HD] = result[:, g * SPAN : (g + 1) * SPAN].T.astype(o_ref.dtype)


def rows_of(ref, span):
    return ref.at[pl.ds(pl.multiple_of(span * SPAN, SPAN), SPAN)]


def near_kernel(at, offset, n_kv, *refs):
    t_ref, q_ref = refs[:2]
    pieces = refs[2 : 2 + n_kv]
    acc_ref, m_ref, kv_ref, sems = refs[2 + n_kv :]
    fetch(
        at, t_ref, pieces, range(n_kv),
        lambda i: kv_ref.at[pl.ds(t_ref[at.bases + i], pieces[i].shape[0])], sems, (),
    )

    def span(step, carry):
        local = t_ref[at.sequence + offset + step]
        rank = t_ref[at.near_rank + t_ref[at.first] + local]
        attend(t_ref, at.near_list, rank, rows_of(q_ref, local), kv_ref, acc_ref.at[step], m_ref.at[step])
        return carry

    lax.fori_loop(0, acc_ref.shape[0], span, 0)


def far_kernel(at, offset, skip, n_kv, n_far, n_out, *refs):
    t_ref, q_ref, acc_in, m_in = refs[:4]
    pieces = refs[4 : 4 + n_kv]
    o_refs = refs[4 + n_kv : 4 + n_kv + n_out]
    acc_ref, run_ref, kv_ref, span_ref, sems = refs[4 + n_kv + n_out :]
    far = range(n_kv - n_far, n_kv)
    fetch(at, t_ref, pieces, far, lambda i: kv_ref, sems, far)

    def span(step, carry):
        local = t_ref[at.sequence + offset + step]
        stored = t_ref[at.first] + local
        query = rows_of(q_ref, local)
        count = t_ref[at.far_rank + stored]

        @pl.when(count == 0)
        def _():
            acc_ref[...] = acc_in[skip + step]

        for size in range(1, 1 + kv_ref.shape[0]):

            @pl.when(count == size)
            def _(size=size):
                slots = [t_ref[at.far_list + t] - t_ref[at.far_first] for t in range(size)]
                keys, values = gather(kv_ref, slots)
                weights = jnp.exp2(scores(keys, query) - m_in[skip + step, :1])
                acc_ref[...] = acc_in[skip + step] + blend(values, weights)

        recheck(at, t_ref, t_ref[at.order + stored], query, pieces, acc_ref, run_ref, span_ref, sems.at[0])
        for index, o_ref in enumerate(o_refs):

            @pl.when(step == index)
            def _(o_ref=o_ref):
                conclude(acc_ref, o_ref)

        return carry

    lax.fori_loop(0, n_out, span, 0)


def whole_kernel(at, offset, n_kv, n_far, count, *refs):
    t_ref, q_ref = refs[:2]
    pieces = refs[2 : 2 + n_kv]
    o_refs = refs[2 + n_kv : -6]
    acc_ref, m_ref, run_ref, kv_ref, span_ref, sems = refs[-6:]
    fetch(
        at, t_ref, pieces, range(n_kv),
        lambda i: kv_ref.at[pl.ds(t_ref[at.bases + i], pieces[i].shape[0])], sems, range(n_kv - n_far, n_kv),
    )

    def span(step, carry):
        local = t_ref[at.sequence + offset + step]
        p = t_ref[at.order + t_ref[at.first] + local]
        query = rows_of(q_ref, local)
        attend(t_ref, at.all_list, p, query, kv_ref, acc_ref, m_ref)
        recheck(at, t_ref, p, query, pieces, acc_ref, run_ref, span_ref, sems.at[0])
        if len(o_refs) == 1:
            conclude(acc_ref, rows_of(o_refs[0], local))
        else:
            for index, o_ref in enumerate(o_refs):

                @pl.when(step == index)
                def _(o_ref=o_ref):
                    conclude(acc_ref, o_ref)

        return carry

    lax.fori_loop(0, count, span, 0)


def attention(q, near, far, near_bases, far_bases, far_first, first_span, span_order, sequence):
    q_spans = q.shape[0] // SPAN
    spans = span_order.shape[0]
    at = Table(spans)
    numbers = jnp.arange(spans, dtype=jnp.int32)
    if far:
        is_far = jnp.logical_and(numbers >= far_first, numbers < far_first + far[0].shape[0])
    else:
        is_far = numbers < 0
    head = jnp.stack([first_span, far_first, *near_bases, *far_bases]).astype(jnp.int32)
    head = jnp.pad(head, (0, at.order - head.shape[0]))
    near_lists = listing(span_order, jnp.logical_not(is_far))
    far_lists = listing(span_order, is_far)
    all_list = listing(span_order, numbers >= 0)[1]
    table = jnp.concatenate([head, span_order, *near_lists, *far_lists, all_list, sequence])
    elements = q.shape[0] * GROUP * spans * SPAN // 2
    n_kv = len(near) + len(far)
    smem, vmem = (pl.BlockSpec(memory_space=space) for space in (pltpu.SMEM, pltpu.VMEM))
    acc_like = pltpu.VMEM((HD + EXTRA, ROWS), jnp.float32)
    m_like = pltpu.VMEM((8, ROWS), jnp.float32)
    kv_like = pltpu.VMEM((spans, SPAN + HD, SPAN), jnp.bfloat16)
    span_like = pltpu.VMEM((SPAN + HD, SPAN), jnp.bfloat16)

    def call(kernel, name, operands, pieces, out_shape, scratch_shapes, part):
        return pl.pallas_call(
            kernel,
            in_specs=[smem] + [vmem] * (len(operands) - 1 + len(pieces)),
            out_specs=[vmem] * len(out_shape),
            out_shape=out_shape,
            scratch_shapes=[*scratch_shapes, pltpu.SemaphoreType.DMA((n_kv,))],
            compiler_params=pltpu.CompilerParams(vmem_limit_bytes=VMEM),
            cost_estimate=pl.CostEstimate(
                flops=int(8 * HD * elements * part),
                bytes_accessed=int(4 * q.size * part) + 4 * spans * SPAN * HD,
                transcendentals=int(elements * part),
            ),
            name=name,
        )(*operands, *pieces)

    def begin(offset, count, q):
        shapes = [
            jax.ShapeDtypeStruct((count, HD + EXTRA, ROWS), jnp.float32),
            jax.ShapeDtypeStruct((count, 8, ROWS), jnp.float32),
        ]
        kernel = functools.partial(near_kernel, at, offset, len(near))
        return call(kernel, "near", (table, q), near, shapes, [kv_like], 0.75 * count / q_spans)

    def finish(begun, begun_at, offset, count):
        shapes = [jax.ShapeDtypeStruct((SPAN, GROUP * HD), q.dtype)] * count
        kernel = functools.partial(far_kernel, at, offset, offset - begun_at, n_kv, len(far), count)
        scratch = [acc_like, m_like, pltpu.VMEM(far[0].shape, jnp.bfloat16), span_like]
        return call(kernel, "far", (table, q, *begun), near + far, shapes, scratch, 0.25 * count / q_spans)

    def whole(offset, count, q, apart):
        if apart:
            shapes = [jax.ShapeDtypeStruct((SPAN, GROUP * HD), q.dtype)] * count
        else:
            shapes = [jax.ShapeDtypeStruct(q.shape, q.dtype)]
        kernel = functools.partial(whole_kernel, at, offset, n_kv, len(far), count)
        scratch = [acc_like, m_like, m_like, kv_like, span_like]
        return call(kernel, "whole", (table, q), near + far, shapes, scratch, count / q_spans)

    return begin, finish, whole


def unpack_kernel(me_ref, *refs):
    parts, (o_ref, sems) = refs[:-2], refs[-2:]
    copies = []
    for index, part in enumerate(parts):
        column = pl.multiple_of((me_ref[0] ^ index) * GROUP * HD, GROUP * HD)
        copies.append(pltpu.make_async_copy(part, o_ref.at[:, pl.ds(column, GROUP * HD)], sems.at[index]))
    for copy in copies:
        copy.start()
    for copy in copies:
        copy.wait()


def to_token_owners(q, begin, finish, whole, me):
    parts = [None] * KVH

    def send(steps, finished):
        for step, done in zip(steps, finished):
            if step:
                done = lax.ppermute(done, GROUP_AXES, [(i, i ^ step) for i in range(KVH)])
            parts[step] = done

    begun = begin(0, sum(map(len, AWAY)), q)
    offset = 0
    for steps in AWAY:
        finished = finish(begun, 0, offset, len(steps))
        send(steps, finished)
        offset += len(steps)
    q, _ = lax.optimization_barrier((q, (finished, [parts[step] for step in AWAY[0]])))
    send(HOME, whole(offset, len(HOME), q, True))
    return pl.pallas_call(
        unpack_kernel,
        in_specs=[pl.BlockSpec(memory_space=pltpu.SMEM)] + [pl.BlockSpec(memory_space=pltpu.VMEM)] * KVH,
        out_specs=pl.BlockSpec(memory_space=pl.ANY),
        out_shape=jax.ShapeDtypeStruct((SPAN, HQ * HD), parts[0].dtype),
        scratch_shapes=[pltpu.SemaphoreType.DMA((KVH,))],
        compiler_params=pltpu.CompilerParams(vmem_limit_bytes=VMEM),
        name="unpack",
    )(me.reshape(1), *parts)


def pack_kernel(k_ref, v_ref, o_ref):
    for h in range(KVH):
        o_ref[h, :SPAN] = k_ref[:, h * HD : (h + 1) * HD]
        o_ref[h, SPAN:] = v_ref[:, h * HD : (h + 1) * HD].T


def to_head_owners(key_rows, value_rows):
    rows = key_rows.shape[0]
    exchange = functools.partial(
        lax.all_to_all, axis_name=GROUP_AXES, split_axis=0, concat_axis=0, tiled=False
    )
    if rows == SPAN:
        packed = pl.pallas_call(
            pack_kernel, out_shape=jax.ShapeDtypeStruct((KVH, SPAN + HD, SPAN), key_rows.dtype), name="pack"
        )(key_rows, value_rows)
        return exchange(packed)
    packed = jnp.concatenate([key_rows.reshape(rows, KVH, HD), value_rows.reshape(rows, KVH, HD)], 2)
    own = exchange(packed.transpose(1, 0, 2)).reshape(KVH * rows // SPAN, SPAN, 2 * HD)
    return jnp.concatenate([own[:, :, :HD], own[:, :, HD:].transpose(0, 2, 1)], 1)


def shards(outer, queries, key_rows, value_rows, span_order):
    rows = queries.shape[0]
    place = lax.axis_index("outer")
    group_rows = KVH * rows
    group_spans = group_rows // SPAN
    own = to_head_owners(key_rows, value_rows)
    q = queries.reshape(rows, KVH, GROUP * HD).transpose(1, 0, 2)
    q = lax.all_to_all(q, GROUP_AXES, split_axis=0, concat_axis=0, tiled=False).reshape(group_rows, GROUP * HD)
    if outer == 4:
        up = lax.ppermute(own, "outer", [(i, (i + 1) % outer) for i in range(outer)])
        down = lax.ppermute(own, "outer", [(i, (i - 1) % outer) for i in range(outer)])
        far_up = lax.ppermute(up, "outer", [(1, 2), (2, 3)])
        far_down = lax.ppermute(down, "outer", [(1, 0), (2, 1)])
        near = [own, up, down]
        near_bases = [(place + step) % outer * group_spans for step in (0, outer - 1, 1)]
        far = [far_up, far_down]
        far_first = (place + 2) % outer * group_spans
        far_bases = [jnp.where(place >= 2, far_first, -1), jnp.where(place < 2, far_first, -1)]
    else:
        near = [lax.all_gather(own, "outer", axis=0, tiled=True)]
        near_bases = [jnp.int32(0)]
        far, far_bases, far_first = [], [], jnp.int32(0)
    me = lax.axis_index(GROUP_AXES).astype(jnp.int32)
    apart = rows == SPAN and outer == 4
    if apart:
        sequence = jnp.stack([me ^ step for steps in (*AWAY, HOME) for step in steps])
    else:
        sequence = jnp.arange(group_spans, dtype=jnp.int32)
    first_span = place * group_spans
    steps = attention(q, near, far, near_bases, far_bases, far_first, first_span, span_order, sequence)
    if apart:
        return to_token_owners(q, *steps, me)
    out = steps[-1](0, group_spans, q, False)[0]
    out = lax.all_to_all(out.reshape(KVH, rows, GROUP * HD), GROUP_AXES, split_axis=0, concat_axis=0, tiled=False)
    return out.transpose(1, 0, 2).reshape(rows, HQ * HD)


def solution(mesh):
    ctx, head = mesh.devices.shape
    inner = KVH // head
    split = Mesh(mesh.devices.reshape(ctx // inner, inner, head), ("outer", "inner", "head"))
    spec = P(("outer", "inner", "head"), None)
    return jax.shard_map(
        functools.partial(shards, ctx // inner),
        mesh=split,
        in_specs=(spec, spec, spec, P()),
        out_specs=spec,
        check_vma=False,
    )
```

profile of v0, /device:TPU:19, one launch (start us, length us, event | category | flops | bytes accessed | tf_op | source)
XLA Modules:
  0.0 99.1 jit_solution(6176533875587970460)
XLA Ops:
  0.0 0.0 copy-start
  0.0 2.1 %pack.1 = bf16[8,256,128]{2,1,0:T(8,128)(2,1)} custom-call(bf16[128,1024]{1,0:T(8,128)(2,1)} %k_ref.1, bf16[128,1024]{1,0:T(8,128)(2,1)} %v_ref.1), custom_call_target="tpu_custom_call" | custom-call | tf_op jit(solution)/shard_map/pack/pallas_call | solution.py:358
  2.1 4.6 %all-to-all-start.1 = ((bf16[8,256,128]{2,1,0:T(8,128)(2,1)}), bf16[8,256,128]{2,1,0:T(8,128)(2,1)S(1)}, u32[]{:S(2)}, u32[]{:S(2)}) async-start(bf16[8,256,128]{2,1,0:T(8,128)(2,1)} %pack.1), calls=%async_computation.1 | async-start | bytes 1048576 | tf_op jit(solution)/shard_map/all_to_all | solution.py:361
  6.7 0.0 copy-done
  6.7 1.6 %copy.9 = bf16[16,8,8,1024]{3,2,0,1:T(8,128)(2,1)} copy(bf16[16,8,8,1024]{3,2,1,0:T(8,128)(2,1)S(1)} %bitcast.28) | data formatting | bytes 4194304 | tf_op jit(solution)/shard_map/reshape | solution.py:373
  8.2 6.2 %all-to-all-done.1.refs_2_.refs_4_ = bf16[8,256,128]{2,1,0:T(8,128)(2,1)S(1)} async-done(((bf16[8,256,128]{2,1,0:T(8,128)(2,1)}), bf16[8,256,128]{2,1,0:T(8,128)(2,1)S(1)}, u32[]{:S(2)}, u32[]{:S(2)}) %all-to-all-start.1) | async-done | bytes 524320 | tf_op jit(solution)/shard_map/all_to_all | solution.py:361
  14.4 0.0 copy-start.1
  14.4 5.1 %all-to-all-start = ((bf16[8,128,1024]{2,1,0:T(8,128)(2,1)}), bf16[8,128,1024]{2,1,0:T(8,128)(2,1)S(1)}, u32[]{:S(2)}, u32[]{:S(2)}) async-start(bf16[8,128,1024]{2,1,0:T(8,128)(2,1)} %bitcast.27), calls=%async_computation | async-start | bytes 4194304 | tf_op jit(solution)/shard_map/all_to_all | solution.py:374
  19.6 1.3 %collective-permute-start = (bf16[8,256,128]{2,1,0:T(8,128)(2,1)S(1)}, bf16[8,256,128]{2,1,0:T(8,128)(2,1)S(1)}, u32[]{:S(2)}, u32[]{:S(2)}) collective-permute-start(bf16[8,256,128]{2,1,0:T(8,128)(2,1)S(1)} %all-to-all-done.1.refs_2_.refs_4_), channel_id=1, source_target_pairs={{0,8},{8,16},{16,24},{24,0},{1,9},{9,17},{17,25},{25,1},{2,10},{10... | collective-permute-start | bytes 1572872 | tf_op jit(solution)/shard_map/ppermute | solution.py:376
  20.9 0.2 collective-permute-start.1
  21.0 0.1 stack.53
  21.1 0.0 copy-done.1
  21.2 0.2 fusion
  21.4 0.1 select_reduce_fusion
  21.5 0.1 select_reduce_fusion.1
  21.6 0.1 concatenate.3.refs_0_
  21.7 11.1 %collective-permute-done.refs_3_.refs_5_ = bf16[8,256,128]{2,1,0:T(8,128)(2,1)S(1)} collective-permute-done((bf16[8,256,128]{2,1,0:T(8,128)(2,1)S(1)}, bf16[8,256,128]{2,1,0:T(8,128)(2,1)S(1)}, u32[]{:S(2)}, u32[]{:S(2)}) %collective-permute-start) | collective-permute-done | bytes 524320 | tf_op jit(solution)/shard_map/ppermute | solution.py:376
  32.8 3.3 %collective-permute-start.2 = (bf16[8,256,128]{2,1,0:T(8,128)(2,1)S(1)}, bf16[8,256,128]{2,1,0:T(8,128)(2,1)}, u32[]{:S(2)}, u32[]{:S(2)}) collective-permute-start(bf16[8,256,128]{2,1,0:T(8,128)(2,1)S(1)} %collective-permute-done.refs_3_.refs_5_), channel_id=1, source_target_pairs={{8,16},{16,24},{9,17},{17,25},{10,18},{18,26},{11,19},{19,27},{12,... | collective-permute-start | bytes 1572872 | tf_op jit(solution)/shard_map/ppermute | solution.py:378
  36.1 7.9 %collective-permute-done.1.refs_4_.refs_6_ = bf16[8,256,128]{2,1,0:T(8,128)(2,1)} collective-permute-done((bf16[8,256,128]{2,1,0:T(8,128)(2,1)S(1)}, bf16[8,256,128]{2,1,0:T(8,128)(2,1)}, u32[]{:S(2)}, u32[]{:S(2)}) %collective-permute-start.1) | collective-permute-done | bytes 524320 | tf_op jit(solution)/shard_map/ppermute | solution.py:377
  44.0 4.5 %collective-permute-start.3 = (bf16[8,256,128]{2,1,0:T(8,128)(2,1)}, bf16[8,256,128]{2,1,0:T(8,128)(2,1)}, u32[]{:S(2)}, u32[]{:S(2)}) collective-permute-start(bf16[8,256,128]{2,1,0:T(8,128)(2,1)} %collective-permute-done.1.refs_4_.refs_6_), channel_id=1, source_target_pairs={{8,0},{16,8},{9,1},{17,9},{10,2},{18,10},{11,3},{19,11},{12,4},{20... | collective-permute-start | bytes 1572872 | tf_op jit(solution)/shard_map/ppermute | solution.py:379
  48.5 0.0 all-to-all-done
  48.5 14.7 %near.1 = (f32[6,144,1024]{2,1,0:T(8,128)S(1)}, f32[6,8,1024]{2,1,0:T(8,128)S(1)}) custom-call(s32[216]{0:T(256)S(1)} %concatenate.3.refs_0_, bf16[1024,1024]{1,0:T(8,128)(2,1)S(1)} %bitcast.23, bf16[8,256,128]{2,1,0:T(8,128)(2,1)S(1)} %all-to-all-done.1.refs_2_.refs_4_, bf16[8,256,128]{2,1,0:T(8,128)(2,1)S(1)} %collective-permute-done.refs_3_.refs_5_, ...), custom_call_target="tpu_custom_call" | custom-call | flops 9663676416 | bytes 4456448 | tf_op jit(solution)/shard_map/near/pallas_call | solution.py:265
  63.2 0.0 collective-permute-done.2.refs_7_.refs_5_
  63.2 0.0 collective-permute-done.3.refs_8_.refs_6_
  63.2 3.7 %far.3 = (bf16[128,1024]{1,0:T(8,128)(2,1)S(1)}, bf16[128,1024]{1,0:T(8,128)(2,1)S(1)}) custom-call(s32[216]{0:T(256)S(1)} %concatenate.3.refs_0_, bf16[1024,1024]{1,0:T(8,128)(2,1)S(1)} %bitcast.24, f32[6,144,1024]{2,1,0:T(8,128)S(1)} %get-tuple-element.16.refs_2_, f32[6,8,1024]{2,1,0:T(8,128)S(1)} %get-tuple-element.17.refs_3_, ...), custom_call_target="tpu_custom_call" | custom-call | flops 1073741824 | bytes 2359296 | tf_op jit(solution)/shard_map/far/pallas_call | solution.py:265
  66.9 4.2 %collective-permute-start.4 = (bf16[128,1024]{1,0:T(8,128)(2,1)S(1)}, bf16[128,1024]{1,0:T(8,128)(2,1)S(1)}, u32[]{:S(2)}, u32[]{:S(2)}) collective-permute-start(bf16[128,1024]{1,0:T(8,128)(2,1)S(1)} %get-tuple-element.22), channel_id=1, source_target_pairs={{0,5},{1,4},{2,7},{3,6},{4,1},{5,0},{6,3},{7,2},{8,13},{9,12},{10,... | collective-permute-start | bytes 786440 | tf_op jit(solution)/shard_map/ppermute | solution.py:324
  71.1 4.1 %collective-permute-start.5 = (bf16[128,1024]{1,0:T(8,128)(2,1)S(1)}, bf16[128,1024]{1,0:T(8,128)(2,1)S(1)}, u32[]{:S(2)}, u32[]{:S(2)}) collective-permute-start(bf16[128,1024]{1,0:T(8,128)(2,1)S(1)} %get-tuple-element.23), channel_id=1, source_target_pairs={{0,7},{1,6},{2,5},{3,4},{4,3},{5,2},{6,1},{7,0},{8,15},{9,14},{10,... | collective-permute-start | bytes 786440 | tf_op jit(solution)/shard_map/ppermute | solution.py:324
  75.2 6.6 %far.2 = (bf16[128,1024]{1,0:T(8,128)(2,1)S(1)}, bf16[128,1024]{1,0:T(8,128)(2,1)S(1)}, bf16[128,1024]{1,0:T(8,128)(2,1)S(1)}, bf16[128,1024]{1,0:T(8,128)(2,1)S(1)}) custom-call(s32[216]{0:T(256)S(1)} %concatenate.3.refs_0_, bf16[1024,1024]{1,0:T(8,128)(2,1)S(1)} %bitcast.25, f32[6,144,1024]{2,1,0:T(8,128)S(1)} %get-tuple-element.16.refs_2_, ...), custom_call_target="tpu_custom_call" | custom-call | flops 2147483648 | bytes 2621440 | tf_op jit(solution)/shard_map/far/pallas_call | solution.py:265
  81.8 0.1 collective-permute-start.10
  81.9 0.3 collective-permute-start.6
  82.2 2.9 %collective-permute-start.8 = (bf16[128,1024]{1,0:T(8,128)(2,1)S(1)}, bf16[128,1024]{1,0:T(8,128)(2,1)S(1)}, u32[]{:S(2)}, u32[]{:S(2)}) collective-permute-start(bf16[128,1024]{1,0:T(8,128)(2,1)S(1)} %get-tuple-element.20), channel_id=1, source_target_pairs={{0,3},{1,2},{2,1},{3,0},{4,7},{5,6},{6,5},{7,4},{8,11},{9,10},{10,... | collective-permute-start | bytes 786440 | tf_op jit(solution)/shard_map/ppermute | solution.py:324
  85.0 0.0 collective-permute-done.4.refs_5_
  85.0 0.3 collective-permute-start.9
  85.4 0.0 collective-permute-done.5.refs_7_
  85.4 10.4 %whole.1 = (bf16[128,1024]{1,0:T(8,128)(2,1)S(1)}, bf16[128,1024]{1,0:T(8,128)(2,1)S(1)}) custom-call(s32[216]{0:T(256)S(1)} %concatenate.3.refs_0_, bf16[1024,1024]{1,0:T(8,128)(2,1)S(1)} %bitcast.26, bf16[8,256,128]{2,1,0:T(8,128)(2,1)S(1)} %all-to-all-done.1.refs_2_.refs_4_, bf16[8,256,128]{2,1,0:T(8,128)(2,1)S(1)} %collective-permute-done.refs_3_.refs_5_, ...), custom_call_target="tpu_custom_call" | custom-call | flops 4294967296 | bytes 3145728 | tf_op jit(solution)/shard_map/whole/pallas_call | solution.py:265
  95.8 0.6 collective-permute-start.7
  96.4 0.0 collective-permute-done.10.refs_6_
  96.4 0.0 collective-permute-done.6.refs_1_
  96.4 0.0 collective-permute-done.8.refs_3_
  96.4 0.0 collective-permute-done.9.refs_4_
  96.4 1.1 %collective-permute-done.7.refs_2_ = bf16[128,1024]{1,0:T(8,128)(2,1)S(1)} collective-permute-done((bf16[128,1024]{1,0:T(8,128)(2,1)S(1)}, bf16[128,1024]{1,0:T(8,128)(2,1)S(1)}, u32[]{:S(2)}, u32[]{:S(2)}) %collective-permute-start.7) | collective-permute-done | bytes 262176 | tf_op jit(solution)/shard_map/ppermute | solution.py:324
  97.6 1.4 %unpack.1 = bf16[128,8192]{1,0:T(8,128)(2,1)} custom-call(s32[1]{0:T(128)} %bitcast.me_ref, bf16[128,1024]{1,0:T(8,128)(2,1)S(1)} %get-tuple-element.25.refs_0_, bf16[128,1024]{1,0:T(8,128)(2,1)S(1)} %collective-permute-done.6.refs_1_, bf16[128,1024]{1,0:T(8,128)(2,1)S(1)} %collective-permute-done.7.refs_2_, ...), custom_call_target="tpu_custom_call" | custom-call | tf_op jit(solution)/shard_map/unpack/pallas_call | solution.py:335
  (2 shorter events, 0.0 us)
Async XLA Ops:
  0.0 6.7 %copy-start = (bf16[128,8192]{1,0:T(8,128)(2,1)S(1)}, bf16[128,8192]{1,0:T(8,128)(2,1)}, u32[]{:S(2)}) copy-start(bf16[128,8192]{1,0:T(8,128)(2,1)} %param.4) | copy-start | bytes 6291460
  2.1 12.3 %all-to-all-start.1 = ((bf16[8,256,128]{2,1,0:T(8,128)(2,1)}), bf16[8,256,128]{2,1,0:T(8,128)(2,1)S(1)}, u32[]{:S(2)}, u32[]{:S(2)}) async-start(bf16[8,256,128]{2,1,0:T(8,128)(2,1)} %pack.1), calls=%async_computation.1 | async-start | bytes 1048576 | tf_op jit(solution)/shard_map/all_to_all | solution.py:361
  14.4 6.7 %copy-start.1 = (s32[32]{0:T(128)S(1)}, s32[32]{0:T(128)}, u32[]{:S(2)}) copy-start(s32[32]{0:T(128)} %param.7) | copy-start | bytes 388
  14.4 34.0 %all-to-all-start = ((bf16[8,128,1024]{2,1,0:T(8,128)(2,1)}), bf16[8,128,1024]{2,1,0:T(8,128)(2,1)S(1)}, u32[]{:S(2)}, u32[]{:S(2)}) async-start(bf16[8,128,1024]{2,1,0:T(8,128)(2,1)} %bitcast.27), calls=%async_computation | async-start | bytes 4194304 | tf_op jit(solution)/shard_map/all_to_all | solution.py:374
  19.6 13.3 %collective-permute-start = (bf16[8,256,128]{2,1,0:T(8,128)(2,1)S(1)}, bf16[8,256,128]{2,1,0:T(8,128)(2,1)S(1)}, u32[]{:S(2)}, u32[]{:S(2)}) collective-permute-start(bf16[8,256,128]{2,1,0:T(8,128)(2,1)S(1)} %all-to-all-done.1.refs_2_.refs_4_), channel_id=1, source_target_pairs={{0,8},{8,16},{16,24},{24,0},{1,9},{9,17},{17,25},{25,1},{2,10},{10... | collective-permute-start | bytes 1572872 | tf_op jit(solution)/shard_map/ppermute | solution.py:376
  20.9 23.1 %collective-permute-start.1 = (bf16[8,256,128]{2,1,0:T(8,128)(2,1)S(1)}, bf16[8,256,128]{2,1,0:T(8,128)(2,1)}, u32[]{:S(2)}, u32[]{:S(2)}) collective-permute-start(bf16[8,256,128]{2,1,0:T(8,128)(2,1)S(1)} %all-to-all-done.1.refs_2_.refs_4_), channel_id=1, source_target_pairs={{0,24},{8,0},{16,8},{24,16},{1,25},{9,1},{17,9},{25,17},{2,26},{10... | collective-permute-start | bytes 1572872 | tf_op jit(solution)/shard_map/ppermute | solution.py:377
  32.8 30.4 %collective-permute-start.2 = (bf16[8,256,128]{2,1,0:T(8,128)(2,1)S(1)}, bf16[8,256,128]{2,1,0:T(8,128)(2,1)}, u32[]{:S(2)}, u32[]{:S(2)}) collective-permute-start(bf16[8,256,128]{2,1,0:T(8,128)(2,1)S(1)} %collective-permute-done.refs_3_.refs_5_), channel_id=1, source_target_pairs={{8,16},{16,24},{9,17},{17,25},{10,18},{18,26},{11,19},{19,27},{12,... | collective-permute-start | bytes 1572872 | tf_op jit(solution)/shard_map/ppermute | solution.py:378
  44.0 19.2 %collective-permute-start.3 = (bf16[8,256,128]{2,1,0:T(8,128)(2,1)}, bf16[8,256,128]{2,1,0:T(8,128)(2,1)}, u32[]{:S(2)}, u32[]{:S(2)}) collective-permute-start(bf16[8,256,128]{2,1,0:T(8,128)(2,1)} %collective-permute-done.1.refs_4_.refs_6_), channel_id=1, source_target_pairs={{8,0},{16,8},{9,1},{17,9},{10,2},{18,10},{11,3},{19,11},{12,4},{20... | collective-permute-start | bytes 1572872 | tf_op jit(solution)/shard_map/ppermute | solution.py:379
  66.9 18.1 %collective-permute-start.4 = (bf16[128,1024]{1,0:T(8,128)(2,1)S(1)}, bf16[128,1024]{1,0:T(8,128)(2,1)S(1)}, u32[]{:S(2)}, u32[]{:S(2)}) collective-permute-start(bf16[128,1024]{1,0:T(8,128)(2,1)S(1)} %get-tuple-element.22), channel_id=1, source_target_pairs={{0,5},{1,4},{2,7},{3,6},{4,1},{5,0},{6,3},{7,2},{8,13},{9,12},{10,... | collective-permute-start | bytes 786440 | tf_op jit(solution)/shard_map/ppermute | solution.py:324
  71.1 14.2 %collective-permute-start.5 = (bf16[128,1024]{1,0:T(8,128)(2,1)S(1)}, bf16[128,1024]{1,0:T(8,128)(2,1)S(1)}, u32[]{:S(2)}, u32[]{:S(2)}) collective-permute-start(bf16[128,1024]{1,0:T(8,128)(2,1)S(1)} %get-tuple-element.23), channel_id=1, source_target_pairs={{0,7},{1,6},{2,5},{3,4},{4,3},{5,2},{6,1},{7,0},{8,15},{9,14},{10,... | collective-permute-start | bytes 786440 | tf_op jit(solution)/shard_map/ppermute | solution.py:324
  81.8 14.6 %collective-permute-start.10 = (bf16[128,1024]{1,0:T(8,128)(2,1)S(1)}, bf16[128,1024]{1,0:T(8,128)(2,1)S(1)}, u32[]{:S(2)}, u32[]{:S(2)}) collective-permute-start(bf16[128,1024]{1,0:T(8,128)(2,1)S(1)} %get-tuple-element.21), channel_id=1, source_target_pairs={{0,6},{1,7},{2,4},{3,5},{4,2},{5,3},{6,0},{7,1},{8,14},{9,15},{10,... | collective-permute-start | bytes 786440 | tf_op jit(solution)/shard_map/ppermute | solution.py:324
  81.9 14.5 %collective-permute-start.6 = (bf16[128,1024]{1,0:T(8,128)(2,1)S(1)}, bf16[128,1024]{1,0:T(8,128)(2,1)S(1)}, u32[]{:S(2)}, u32[]{:S(2)}) collective-permute-start(bf16[128,1024]{1,0:T(8,128)(2,1)S(1)} %get-tuple-element.18), channel_id=1, source_target_pairs={{0,1},{1,0},{2,3},{3,2},{4,5},{5,4},{6,7},{7,6},{8,9},{9,8},{10,11... | collective-permute-start | bytes 786440 | tf_op jit(solution)/shard_map/ppermute | solution.py:324
  82.2 14.2 %collective-permute-start.8 = (bf16[128,1024]{1,0:T(8,128)(2,1)S(1)}, bf16[128,1024]{1,0:T(8,128)(2,1)S(1)}, u32[]{:S(2)}, u32[]{:S(2)}) collective-permute-start(bf16[128,1024]{1,0:T(8,128)(2,1)S(1)} %get-tuple-element.20), channel_id=1, source_target_pairs={{0,3},{1,2},{2,1},{3,0},{4,7},{5,6},{6,5},{7,4},{8,11},{9,10},{10,... | collective-permute-start | bytes 786440 | tf_op jit(solution)/shard_map/ppermute | solution.py:324
  85.0 11.4 %collective-permute-start.9 = (bf16[128,1024]{1,0:T(8,128)(2,1)S(1)}, bf16[128,1024]{1,0:T(8,128)(2,1)S(1)}, u32[]{:S(2)}, u32[]{:S(2)}) collective-permute-start(bf16[128,1024]{1,0:T(8,128)(2,1)S(1)} %get-tuple-element.19), channel_id=1, source_target_pairs={{0,4},{1,5},{2,6},{3,7},{4,0},{5,1},{6,2},{7,3},{8,12},{9,13},{10,... | collective-permute-start | bytes 786440 | tf_op jit(solution)/shard_map/ppermute | solution.py:324
  95.8 1.8 %collective-permute-start.7 = (bf16[128,1024]{1,0:T(8,128)(2,1)S(1)}, bf16[128,1024]{1,0:T(8,128)(2,1)S(1)}, u32[]{:S(2)}, u32[]{:S(2)}) collective-permute-start(bf16[128,1024]{1,0:T(8,128)(2,1)S(1)} %get-tuple-element.26), channel_id=1, source_target_pairs={{0,2},{1,3},{2,0},{3,1},{4,6},{5,7},{6,4},{7,5},{8,10},{9,11},{10,... | collective-permute-start | bytes 786440 | tf_op jit(solution)/shard_map/ppermute | solution.py:324
where the time goes:
time: 98.2 us; the launch traced here: 99.1 us
  Pallas kernels  38.9 us (40%)
  starting transfers between devices  31.4 us (32%)
  waiting for transfers between devices  26.4 us (27%)
  local copies, waits for them, and re-layouts  1.75 us (2%)
    pallas_call x4, Pallas kernels, call(): pl.pallas_call(kernel, in_specs=[smem] + [vmem] * (len(operands) - 1 + le...  35.4 us
    ppermute x7, starting transfers between devices, send(): done = lax.ppermute(done, GROUP_AXES, [(i, i ^ step) for i in range(KVH)])  12.4 us
    ppermute x1, waiting for transfers between devices, shards(): lax.ppermute(own, 'outer', [(i, (i + 1) % outer) for i in range(outer)])  11.1 us
    ppermute x1, waiting for transfers between devices, shards(): lax.ppermute(own, 'outer', [(i, (i - 1) % outer) for i in range(outer)])  7.87 us
    all_to_all x1, waiting for transfers between devices, to_head_owners(): return exchange(packed)  6.21 us
    all_to_all x1, starting transfers between devices, shards(): lax.all_to_all(q, GROUP_AXES, split_axis=0, concat_axis=0, tiled=False)  5.13 us
    all_to_all x1, starting transfers between devices, to_head_owners(): return exchange(packed)  4.57 us
    ppermute x1, starting transfers between devices, shards(): far_down = lax.ppermute(down, 'outer', [(1, 0), (2, 1)])  4.47 us
  transfers between devices with their start and end apart: 13, of which 4 were waited for; matrix products, arithmetic and copies ran while one was open for 2% of the time, Pallas kernels for 32%

commit v1 on v0

--- a/solution.py
+++ b/solution.py
@@ -71,20 +71,19 @@
         self.sequence = 16 + spans * 6
 
 
-def fetch(at, t_ref, pieces, indices, target_of, sems, optional):
-    def copy_of(index):
-        return pltpu.make_async_copy(pieces[index], target_of(index), sems.at[index])
-
-    for act in ("start", "wait"):
-        for index in indices:
-            if index in optional:
-
-                @pl.when(t_ref[at.bases + index] >= 0)
-                def _(index=index):
-                    getattr(copy_of(index), act)()
-
-            else:
-                getattr(copy_of(index), act)()
+def fetch(pieces, targets, sems):
+    copies = [
+        pltpu.make_async_copy(piece, target, sems.at[index])
+        for index, (piece, target) in enumerate(zip(pieces, targets))
+    ]
+    for copy in copies:
+        copy.start()
+    for copy in copies:
+        copy.wait()
+
+
+def places(at, t_ref, kv_ref, pieces):
+    return [kv_ref.at[pl.ds(t_ref[at.bases + i], piece.shape[0])] for i, piece in enumerate(pieces)]
 
 
 def attend(t_ref, list_at, rank, q_ref, kv_ref, acc_ref, m_ref):
@@ -121,9 +120,9 @@
             base = t_ref[at.bases + index]
 
             def careful(j, carry, piece=piece, base=base):
-                other = t_ref[at.order + jnp.maximum(base, 0) + j]
-
-                @pl.when(jnp.logical_and(base >= 0, other <= p))
+                other = t_ref[at.order + base + j]
+
+                @pl.when(other <= p)
                 def _():
                     copy = pltpu.make_async_copy(piece.at[j], span_ref, sem)
                     copy.start()
@@ -155,10 +154,7 @@
     t_ref, q_ref = refs[:2]
     pieces = refs[2 : 2 + n_kv]
     acc_ref, m_ref, kv_ref, sems = refs[2 + n_kv :]
-    fetch(
-        at, t_ref, pieces, range(n_kv),
-        lambda i: kv_ref.at[pl.ds(t_ref[at.bases + i], pieces[i].shape[0])], sems, (),
-    )
+    fetch(pieces, places(at, t_ref, kv_ref, pieces), sems)
 
     def span(step, carry):
         local = t_ref[at.sequence + offset + step]
@@ -169,13 +165,12 @@
     lax.fori_loop(0, acc_ref.shape[0], span, 0)
 
 
-def far_kernel(at, offset, skip, n_kv, n_far, n_out, *refs):
+def far_kernel(at, offset, skip, n_kv, n_out, *refs):
     t_ref, q_ref, acc_in, m_in = refs[:4]
     pieces = refs[4 : 4 + n_kv]
     o_refs = refs[4 + n_kv : 4 + n_kv + n_out]
     acc_ref, run_ref, kv_ref, span_ref, sems = refs[4 + n_kv + n_out :]
-    far = range(n_kv - n_far, n_kv)
-    fetch(at, t_ref, pieces, far, lambda i: kv_ref, sems, far)
+    fetch(pieces[-1:], [kv_ref], sems)
 
     def span(step, carry):
         local = t_ref[at.sequence + offset + step]
@@ -208,15 +203,12 @@
     lax.fori_loop(0, n_out, span, 0)
 
 
-def whole_kernel(at, offset, n_kv, n_far, count, *refs):
+def whole_kernel(at, offset, n_kv, count, *refs):
     t_ref, q_ref = refs[:2]
     pieces = refs[2 : 2 + n_kv]
     o_refs = refs[2 + n_kv : -6]
     acc_ref, m_ref, run_ref, kv_ref, span_ref, sems = refs[-6:]
-    fetch(
-        at, t_ref, pieces, range(n_kv),
-        lambda i: kv_ref.at[pl.ds(t_ref[at.bases + i], pieces[i].shape[0])], sems, range(n_kv - n_far, n_kv),
-    )
+    fetch(pieces, places(at, t_ref, kv_ref, pieces), sems)
 
     def span(step, carry):
         local = t_ref[at.sequence + offset + step]
@@ -287,7 +279,7 @@
 
     def finish(begun, begun_at, offset, count):
         shapes = [jax.ShapeDtypeStruct((SPAN, GROUP * HD), q.dtype)] * count
-        kernel = functools.partial(far_kernel, at, offset, offset - begun_at, n_kv, len(far), count)
+        kernel = functools.partial(far_kernel, at, offset, offset - begun_at, n_kv, count)
         scratch = [acc_like, m_like, pltpu.VMEM(far[0].shape, jnp.bfloat16), span_like]
         return call(kernel, "far", (table, q, *begun), near + far, shapes, scratch, 0.25 * count / q_spans)
 
@@ -296,7 +288,7 @@
             shapes = [jax.ShapeDtypeStruct((SPAN, GROUP * HD), q.dtype)] * count
         else:
             shapes = [jax.ShapeDtypeStruct(q.shape, q.dtype)]
-        kernel = functools.partial(whole_kernel, at, offset, n_kv, len(far), count)
+        kernel = functools.partial(whole_kernel, at, offset, n_kv, count)
         scratch = [acc_like, m_like, m_like, kv_like, span_like]
         return call(kernel, "whole", (table, q), near + far, shapes, scratch, count / q_spans)
 
@@ -375,13 +367,11 @@
     if outer == 4:
         up = lax.ppermute(own, "outer", [(i, (i + 1) % outer) for i in range(outer)])
         down = lax.ppermute(own, "outer", [(i, (i - 1) % outer) for i in range(outer)])
-        far_up = lax.ppermute(up, "outer", [(1, 2), (2, 3)])
-        far_down = lax.ppermute(down, "outer", [(1, 0), (2, 1)])
+        far = [lax.ppermute(up, "outer", [(i, (i + 1) % outer) for i in range(outer)])]
         near = [own, up, down]
         near_bases = [(place + step) % outer * group_spans for step in (0, outer - 1, 1)]
-        far = [far_up, far_down]
-        far_first = (place + 2) % outer * group_spans
-        far_bases = [jnp.where(place >= 2, far_first, -1), jnp.where(place < 2, far_first, -1)]
+        far_first = (place + outer - 2) % outer * group_spans
+        far_bases = [far_first]
     else:
         near = [lax.all_gather(own, "outer", axis=0, tiled=True)]
         near_bases = [jnp.int32(0)]

time: 98.2 us -> 93.6 us (0.953)
  the two profiles are of different devices: /device:TPU:19 before, /device:TPU:0 now
where the time goes in v1:
time: 93.6 us; the launch traced here: 94.7 us
  Pallas kernels  36.5 us (39%)
  waiting for transfers between devices  32.2 us (34%)
  starting transfers between devices  23.4 us (25%)
  local copies, waits for them, and re-layouts  1.75 us (2%)
    pallas_call x4, Pallas kernels, call(): pl.pallas_call(kernel, in_specs=[smem] + [vmem] * (len(operands) - 1 + le...  33.1 us
    ppermute x1, waiting for transfers between devices, shards(): lax.ppermute(own, 'outer', [(i, (i + 1) % outer) for i in range(outer)])  12.1 us
    ppermute x7, starting transfers between devices, send(): done = lax.ppermute(done, GROUP_AXES, [(i, i ^ step) for i in range(KVH)])  10.6 us
    ppermute x1, waiting for transfers between devices, shards(): lax.ppermute(own, 'outer', [(i, (i - 1) % outer) for i in range(outer)])  10.2 us
    all_to_all x1, waiting for transfers between devices, to_head_owners(): return exchange(packed)  7.7 us
    all_to_all x1, starting transfers between devices, to_head_owners(): return exchange(packed)  5.17 us
    all_to_all x1, starting transfers between devices, shards(): lax.all_to_all(q, GROUP_AXES, split_axis=0, concat_axis=0, tiled=False)  3.74 us
    ppermute x1, starting transfers between devices, shards(): lax.ppermute(own, 'outer', [(i, (i - 1) % outer) for i in range(outer)])  2.25 us
  transfers between devices with their start and end apart: 12, of which 6 were waited for; matrix products, arithmetic and copies ran while one was open for 2% of the time, Pallas kernels for 31%

profile of v1, /device:TPU:0, one launch (start us, length us, event | category | flops | bytes accessed | tf_op | source)
XLA Modules:
  0.0 94.7 jit_solution(17838587428666382670)
XLA Ops:
  0.0 0.0 copy-start
  0.0 2.1 %pack.1 = bf16[8,256,128]{2,1,0:T(8,128)(2,1)} custom-call(bf16[128,1024]{1,0:T(8,128)(2,1)} %k_ref.1, bf16[128,1024]{1,0:T(8,128)(2,1)} %v_ref.1), custom_call_target="tpu_custom_call" | custom-call | tf_op jit(solution)/shard_map/pack/pallas_call | solution.py:350
  2.1 5.2 %all-to-all-start.1 = ((bf16[8,256,128]{2,1,0:T(8,128)(2,1)}), bf16[8,256,128]{2,1,0:T(8,128)(2,1)S(1)}, u32[]{:S(2)}, u32[]{:S(2)}) async-start(bf16[8,256,128]{2,1,0:T(8,128)(2,1)} %pack.1), calls=%async_computation.1 | async-start | bytes 1048576 | tf_op jit(solution)/shard_map/all_to_all | solution.py:353
  7.3 0.0 copy-done
  7.3 1.6 %copy.9 = bf16[16,8,8,1024]{3,2,0,1:T(8,128)(2,1)} copy(bf16[16,8,8,1024]{3,2,1,0:T(8,128)(2,1)S(1)} %bitcast.26) | data formatting | bytes 4194304 | tf_op jit(solution)/shard_map/reshape | solution.py:365
  8.8 7.7 %all-to-all-done.1.refs_2_.refs_4_ = bf16[8,256,128]{2,1,0:T(8,128)(2,1)S(1)} async-done(((bf16[8,256,128]{2,1,0:T(8,128)(2,1)}), bf16[8,256,128]{2,1,0:T(8,128)(2,1)S(1)}, u32[]{:S(2)}, u32[]{:S(2)}) %all-to-all-start.1) | async-done | bytes 524320 | tf_op jit(solution)/shard_map/all_to_all | solution.py:353
  16.5 0.0 copy-start.1
  16.5 3.7 %all-to-all-start = ((bf16[8,128,1024]{2,1,0:T(8,128)(2,1)}), bf16[8,128,1024]{2,1,0:T(8,128)(2,1)S(1)}, u32[]{:S(2)}, u32[]{:S(2)}) async-start(bf16[8,128,1024]{2,1,0:T(8,128)(2,1)} %bitcast.25), calls=%async_computation | async-start | bytes 4194304 | tf_op jit(solution)/shard_map/all_to_all | solution.py:366
  20.3 1.6 %collective-permute-start = (bf16[8,256,128]{2,1,0:T(8,128)(2,1)S(1)}, bf16[8,256,128]{2,1,0:T(8,128)(2,1)S(1)}, u32[]{:S(2)}, u32[]{:S(2)}) collective-permute-start(bf16[8,256,128]{2,1,0:T(8,128)(2,1)S(1)} %all-to-all-done.1.refs_2_.refs_4_), channel_id=1, source_target_pairs={{0,8},{8,16},{16,24},{24,0},{1,9},{9,17},{17,25},{25,1},{2,10},{10... | collective-permute-start | bytes 1572872 | tf_op jit(solution)/shard_map/ppermute | solution.py:368
  21.9 2.2 %collective-permute-start.1 = (bf16[8,256,128]{2,1,0:T(8,128)(2,1)S(1)}, bf16[8,256,128]{2,1,0:T(8,128)(2,1)}, u32[]{:S(2)}, u32[]{:S(2)}) collective-permute-start(bf16[8,256,128]{2,1,0:T(8,128)(2,1)S(1)} %all-to-all-done.1.refs_2_.refs_4_), channel_id=1, source_target_pairs={{0,24},{8,0},{16,8},{24,16},{1,25},{9,1},{17,9},{25,17},{2,26},{10... | collective-permute-start | bytes 1572872 | tf_op jit(solution)/shard_map/ppermute | solution.py:369
  24.2 0.1 stack.46
  24.3 0.0 copy-done.1
  24.3 0.2 fusion
  24.5 0.1 select_reduce_fusion
  24.6 0.1 select_reduce_fusion.1
  24.7 0.1 concatenate.3.refs_0_
  24.8 12.1 %collective-permute-done.refs_3_.refs_5_ = bf16[8,256,128]{2,1,0:T(8,128)(2,1)S(1)} collective-permute-done((bf16[8,256,128]{2,1,0:T(8,128)(2,1)S(1)}, bf16[8,256,128]{2,1,0:T(8,128)(2,1)S(1)}, u32[]{:S(2)}, u32[]{:S(2)}) %collective-permute-start) | collective-permute-done | bytes 524320 | tf_op jit(solution)/shard_map/ppermute | solution.py:368
  36.9 0.0 collective-permute-start.2
  36.9 10.2 %collective-permute-done.1.refs_4_.refs_6_ = bf16[8,256,128]{2,1,0:T(8,128)(2,1)} collective-permute-done((bf16[8,256,128]{2,1,0:T(8,128)(2,1)S(1)}, bf16[8,256,128]{2,1,0:T(8,128)(2,1)}, u32[]{:S(2)}, u32[]{:S(2)}) %collective-permute-start.1) | collective-permute-done | bytes 524320 | tf_op jit(solution)/shard_map/ppermute | solution.py:369
  47.2 0.0 all-to-all-done
  47.2 12.6 %near.1 = (f32[6,144,1024]{2,1,0:T(8,128)S(1)}, f32[6,8,1024]{2,1,0:T(8,128)S(1)}) custom-call(s32[216]{0:T(256)S(1)} %concatenate.3.refs_0_, bf16[1024,1024]{1,0:T(8,128)(2,1)S(1)} %bitcast.21, bf16[8,256,128]{2,1,0:T(8,128)(2,1)S(1)} %all-to-all-done.1.refs_2_.refs_4_, bf16[8,256,128]{2,1,0:T(8,128)(2,1)S(1)} %collective-permute-done.refs_3_.refs_5_, ...), custom_call_target="tpu_custom_call" | custom-call | flops 9663676416 | bytes 4456448 | tf_op jit(solution)/shard_map/near/pallas_call | solution.py:257
  59.8 0.0 collective-permute-done.2.refs_7_.refs_5_
  59.8 3.8 %far.3 = (bf16[128,1024]{1,0:T(8,128)(2,1)S(1)}, bf16[128,1024]{1,0:T(8,128)(2,1)S(1)}) custom-call(s32[216]{0:T(256)S(1)} %concatenate.3.refs_0_, bf16[1024,1024]{1,0:T(8,128)(2,1)S(1)} %bitcast.22, f32[6,144,1024]{2,1,0:T(8,128)S(1)} %get-tuple-element.16.refs_2_, f32[6,8,1024]{2,1,0:T(8,128)S(1)} %get-tuple-element.17.refs_3_, ...), custom_call_target="tpu_custom_call" | custom-call | flops 1073741824 | bytes 2359296 | tf_op jit(solution)/shard_map/far/pallas_call | solution.py:257
  63.5 5.0 %collective-permute-start.3 = (bf16[128,1024]{1,0:T(8,128)(2,1)S(1)}, bf16[128,1024]{1,0:T(8,128)(2,1)S(1)}, u32[]{:S(2)}, u32[]{:S(2)}) collective-permute-start(bf16[128,1024]{1,0:T(8,128)(2,1)S(1)} %get-tuple-element.22), channel_id=1, source_target_pairs={{0,5},{1,4},{2,7},{3,6},{4,1},{5,0},{6,3},{7,2},{8,13},{9,12},{10,... | collective-permute-start | bytes 786440 | tf_op jit(solution)/shard_map/ppermute | solution.py:316
  68.5 0.0 collective-permute-start.4
  68.5 5.9 %far.2 = (bf16[128,1024]{1,0:T(8,128)(2,1)S(1)}, bf16[128,1024]{1,0:T(8,128)(2,1)S(1)}, bf16[128,1024]{1,0:T(8,128)(2,1)S(1)}, bf16[128,1024]{1,0:T(8,128)(2,1)S(1)}) custom-call(s32[216]{0:T(256)S(1)} %concatenate.3.refs_0_, bf16[1024,1024]{1,0:T(8,128)(2,1)S(1)} %bitcast.23, f32[6,144,1024]{2,1,0:T(8,128)S(1)} %get-tuple-element.16.refs_2_, ...), custom_call_target="tpu_custom_call" | custom-call | flops 2147483648 | bytes 2621440 | tf_op jit(solution)/shard_map/far/pallas_call | solution.py:257
  74.4 2.6 %collective-permute-start.5 = (bf16[128,1024]{1,0:T(8,128)(2,1)S(1)}, bf16[128,1024]{1,0:T(8,128)(2,1)S(1)}, u32[]{:S(2)}, u32[]{:S(2)}) collective-permute-start(bf16[128,1024]{1,0:T(8,128)(2,1)S(1)} %get-tuple-element.18), channel_id=1, source_target_pairs={{0,1},{1,0},{2,3},{3,2},{4,5},{5,4},{6,7},{7,6},{8,9},{9,8},{10,11... | collective-permute-start | bytes 786440 | tf_op jit(solution)/shard_map/ppermute | solution.py:316
  77.0 0.3 collective-permute-start.7
  77.3 2.6 %collective-permute-start.8 = (bf16[128,1024]{1,0:T(8,128)(2,1)S(1)}, bf16[128,1024]{1,0:T(8,128)(2,1)S(1)}, u32[]{:S(2)}, u32[]{:S(2)}) collective-permute-start(bf16[128,1024]{1,0:T(8,128)(2,1)S(1)} %get-tuple-element.19), channel_id=1, source_target_pairs={{0,4},{1,5},{2,6},{3,7},{4,0},{5,1},{6,2},{7,3},{8,12},{9,13},{10,... | collective-permute-start | bytes 786440 | tf_op jit(solution)/shard_map/ppermute | solution.py:316
  79.9 0.0 collective-permute-done.3.refs_5_
  79.9 0.0 collective-permute-start.9
  79.9 0.7 collective-permute-done.4.refs_7_
  80.6 10.9 %whole.1 = (bf16[128,1024]{1,0:T(8,128)(2,1)S(1)}, bf16[128,1024]{1,0:T(8,128)(2,1)S(1)}) custom-call(s32[216]{0:T(256)S(1)} %concatenate.3.refs_0_, bf16[1024,1024]{1,0:T(8,128)(2,1)S(1)} %bitcast.24, bf16[8,256,128]{2,1,0:T(8,128)(2,1)S(1)} %all-to-all-done.1.refs_2_.refs_4_, bf16[8,256,128]{2,1,0:T(8,128)(2,1)S(1)} %collective-permute-done.refs_3_.refs_5_, ...), custom_call_target="tpu_custom_call" | custom-call | flops 4294967296 | bytes 3145728 | tf_op jit(solution)/shard_map/whole/pallas_call | solution.py:257
  91.5 0.1 collective-permute-start.6
  91.6 0.0 collective-permute-done.5.refs_1_
  91.6 0.0 collective-permute-done.7.refs_3_
  91.6 0.0 collective-permute-done.8.refs_4_
  91.6 0.4 collective-permute-done.9.refs_6_
  92.0 1.1 %collective-permute-done.6.refs_2_ = bf16[128,1024]{1,0:T(8,128)(2,1)S(1)} collective-permute-done((bf16[128,1024]{1,0:T(8,128)(2,1)S(1)}, bf16[128,1024]{1,0:T(8,128)(2,1)S(1)}, u32[]{:S(2)}, u32[]{:S(2)}) %collective-permute-start.6) | collective-permute-done | bytes 262176 | tf_op jit(solution)/shard_map/ppermute | solution.py:316
  93.1 1.4 %unpack.1 = bf16[128,8192]{1,0:T(8,128)(2,1)} custom-call(s32[1]{0:T(128)} %bitcast.me_ref, bf16[128,1024]{1,0:T(8,128)(2,1)S(1)} %get-tuple-element.25.refs_0_, bf16[128,1024]{1,0:T(8,128)(2,1)S(1)} %collective-permute-done.5.refs_1_, bf16[128,1024]{1,0:T(8,128)(2,1)S(1)} %collective-permute-done.6.refs_2_, ...), custom_call_target="tpu_custom_call" | custom-call | tf_op jit(solution)/shard_map/unpack/pallas_call | solution.py:327
  (2 shorter events, 0.0 us)
Async XLA Ops:
  0.0 7.3 %copy-start = (bf16[128,8192]{1,0:T(8,128)(2,1)S(1)}, bf16[128,8192]{1,0:T(8,128)(2,1)}, u32[]{:S(2)}) copy-start(bf16[128,8192]{1,0:T(8,128)(2,1)} %param.4) | copy-start | bytes 6291460
  2.1 14.4 %all-to-all-start.1 = ((bf16[8,256,128]{2,1,0:T(8,128)(2,1)}), bf16[8,256,128]{2,1,0:T(8,128)(2,1)S(1)}, u32[]{:S(2)}, u32[]{:S(2)}) async-start(bf16[8,256,128]{2,1,0:T(8,128)(2,1)} %pack.1), calls=%async_computation.1 | async-start | bytes 1048576 | tf_op jit(solution)/shard_map/all_to_all | solution.py:353
  16.5 7.7 %copy-start.1 = (s32[32]{0:T(128)S(1)}, s32[32]{0:T(128)}, u32[]{:S(2)}) copy-start(s32[32]{0:T(128)} %param.7) | copy-start | bytes 388
  16.5 30.6 %all-to-all-start = ((bf16[8,128,1024]{2,1,0:T(8,128)(2,1)}), bf16[8,128,1024]{2,1,0:T(8,128)(2,1)S(1)}, u32[]{:S(2)}, u32[]{:S(2)}) async-start(bf16[8,128,1024]{2,1,0:T(8,128)(2,1)} %bitcast.25), calls=%async_computation | async-start | bytes 4194304 | tf_op jit(solution)/shard_map/all_to_all | solution.py:366
  20.3 16.6 %collective-permute-start = (bf16[8,256,128]{2,1,0:T(8,128)(2,1)S(1)}, bf16[8,256,128]{2,1,0:T(8,128)(2,1)S(1)}, u32[]{:S(2)}, u32[]{:S(2)}) collective-permute-start(bf16[8,256,128]{2,1,0:T(8,128)(2,1)S(1)} %all-to-all-done.1.refs_2_.refs_4_), channel_id=1, source_target_pairs={{0,8},{8,16},{16,24},{24,0},{1,9},{9,17},{17,25},{25,1},{2,10},{10... | collective-permute-start | bytes 1572872 | tf_op jit(solution)/shard_map/ppermute | solution.py:368
  21.9 25.2 %collective-permute-start.1 = (bf16[8,256,128]{2,1,0:T(8,128)(2,1)S(1)}, bf16[8,256,128]{2,1,0:T(8,128)(2,1)}, u32[]{:S(2)}, u32[]{:S(2)}) collective-permute-start(bf16[8,256,128]{2,1,0:T(8,128)(2,1)S(1)} %all-to-all-done.1.refs_2_.refs_4_), channel_id=1, source_target_pairs={{0,24},{8,0},{16,8},{24,16},{1,25},{9,1},{17,9},{25,17},{2,26},{10... | collective-permute-start | bytes 1572872 | tf_op jit(solution)/shard_map/ppermute | solution.py:369
  36.9 22.8 %collective-permute-start.2 = (bf16[8,256,128]{2,1,0:T(8,128)(2,1)S(1)}, bf16[8,256,128]{2,1,0:T(8,128)(2,1)}, u32[]{:S(2)}, u32[]{:S(2)}) collective-permute-start(bf16[8,256,128]{2,1,0:T(8,128)(2,1)S(1)} %collective-permute-done.refs_3_.refs_5_), channel_id=1, source_target_pairs={{0,8},{8,16},{16,24},{24,0},{1,9},{9,17},{17,25},{25,1},{2,10},{10... | collective-permute-start | bytes 1572872 | tf_op jit(solution)/shard_map/ppermute | solution.py:370
  63.5 16.4 %collective-permute-start.3 = (bf16[128,1024]{1,0:T(8,128)(2,1)S(1)}, bf16[128,1024]{1,0:T(8,128)(2,1)S(1)}, u32[]{:S(2)}, u32[]{:S(2)}) collective-permute-start(bf16[128,1024]{1,0:T(8,128)(2,1)S(1)} %get-tuple-element.22), channel_id=1, source_target_pairs={{0,5},{1,4},{2,7},{3,6},{4,1},{5,0},{6,3},{7,2},{8,13},{9,12},{10,... | collective-permute-start | bytes 786440 | tf_op jit(solution)/shard_map/ppermute | solution.py:316
  68.5 12.1 %collective-permute-start.4 = (bf16[128,1024]{1,0:T(8,128)(2,1)S(1)}, bf16[128,1024]{1,0:T(8,128)(2,1)S(1)}, u32[]{:S(2)}, u32[]{:S(2)}) collective-permute-start(bf16[128,1024]{1,0:T(8,128)(2,1)S(1)} %get-tuple-element.23), channel_id=1, source_target_pairs={{0,7},{1,6},{2,5},{3,4},{4,3},{5,2},{6,1},{7,0},{8,15},{9,14},{10,... | collective-permute-start | bytes 786440 | tf_op jit(solution)/shard_map/ppermute | solution.py:316
  74.4 17.2 %collective-permute-start.5 = (bf16[128,1024]{1,0:T(8,128)(2,1)S(1)}, bf16[128,1024]{1,0:T(8,128)(2,1)S(1)}, u32[]{:S(2)}, u32[]{:S(2)}) collective-permute-start(bf16[128,1024]{1,0:T(8,128)(2,1)S(1)} %get-tuple-element.18), channel_id=1, source_target_pairs={{0,1},{1,0},{2,3},{3,2},{4,5},{5,4},{6,7},{7,6},{8,9},{9,8},{10,11... | collective-permute-start | bytes 786440 | tf_op jit(solution)/shard_map/ppermute | solution.py:316
  77.0 14.6 %collective-permute-start.7 = (bf16[128,1024]{1,0:T(8,128)(2,1)S(1)}, bf16[128,1024]{1,0:T(8,128)(2,1)S(1)}, u32[]{:S(2)}, u32[]{:S(2)}) collective-permute-start(bf16[128,1024]{1,0:T(8,128)(2,1)S(1)} %get-tuple-element.20), channel_id=1, source_target_pairs={{0,3},{1,2},{2,1},{3,0},{4,7},{5,6},{6,5},{7,4},{8,11},{9,10},{10,... | collective-permute-start | bytes 786440 | tf_op jit(solution)/shard_map/ppermute | solution.py:316
  77.3 14.3 %collective-permute-start.8 = (bf16[128,1024]{1,0:T(8,128)(2,1)S(1)}, bf16[128,1024]{1,0:T(8,128)(2,1)S(1)}, u32[]{:S(2)}, u32[]{:S(2)}) collective-permute-start(bf16[128,1024]{1,0:T(8,128)(2,1)S(1)} %get-tuple-element.19), channel_id=1, source_target_pairs={{0,4},{1,5},{2,6},{3,7},{4,0},{5,1},{6,2},{7,3},{8,12},{9,13},{10,... | collective-permute-start | bytes 786440 | tf_op jit(solution)/shard_map/ppermute | solution.py:316
  79.9 12.1 %collective-permute-start.9 = (bf16[128,1024]{1,0:T(8,128)(2,1)S(1)}, bf16[128,1024]{1,0:T(8,128)(2,1)S(1)}, u32[]{:S(2)}, u32[]{:S(2)}) collective-permute-start(bf16[128,1024]{1,0:T(8,128)(2,1)S(1)} %get-tuple-element.21), channel_id=1, source_target_pairs={{0,6},{1,7},{2,4},{3,5},{4,2},{5,3},{6,0},{7,1},{8,14},{9,15},{10,... | collective-permute-start | bytes 786440 | tf_op jit(solution)/shard_map/ppermute | solution.py:316
  91.5 1.6 %collective-permute-start.6 = (bf16[128,1024]{1,0:T(8,128)(2,1)S(1)}, bf16[128,1024]{1,0:T(8,128)(2,1)S(1)}, u32[]{:S(2)}, u32[]{:S(2)}) collective-permute-start(bf16[128,1024]{1,0:T(8,128)(2,1)S(1)} %get-tuple-element.26), channel_id=1, source_target_pairs={{0,2},{1,3},{2,0},{3,1},{4,6},{5,7},{6,4},{7,5},{8,10},{9,11},{10,... | collective-permute-start | bytes 786440 | tf_op jit(solution)/shard_map/ppermute | solution.py:316

commit v2 on v1

--- a/solution.py
+++ b/solution.py
@@ -111,33 +111,62 @@
     lax.fori_loop(0, rank // BLOCK, block, 0)
 
 
-def recheck(at, t_ref, p, q_ref, pieces, acc_ref, run_ref, span_ref, sem):
-    @pl.when(jnp.logical_not(jnp.max(acc_ref[HD : HD + 8]) < 1e30))
+def careful(at, t_ref, p, q_ref, pieces, acc_ref, run_ref, span_ref, sem):
+    run_ref[...] = jnp.full_like(run_ref, -1e30)
+    acc_ref[...] = jnp.zeros_like(acc_ref)
+    for index, piece in enumerate(pieces):
+        base = t_ref[at.bases + index]
+
+        def visit(j, carry, piece=piece, base=base):
+            other = t_ref[at.order + base + j]
+
+            @pl.when(other <= p)
+            def _():
+                copy = pltpu.make_async_copy(piece.at[j], span_ref, sem)
+                copy.start()
+                copy.wait()
+                s = scores(span_ref[:SPAN], q_ref)
+                s = jnp.where(other < p, s, causal(s))
+                old = run_ref[...]
+                new = jnp.maximum(old, jnp.max(s, axis=0, keepdims=True))
+                run_ref[...] = new
+                fresh = blend(span_ref[SPAN:], jnp.exp2(s - new[:1]))
+                acc_ref[...] = acc_ref[...] * jnp.exp2(old - new)[:1] + fresh
+
+            return carry
+
+        lax.fori_loop(0, piece.shape[0], visit, 0)
+
+
+def each_span(at, offset, count, t_ref, q_ref, pieces, o_refs, acc_ref, worst_ref, run_ref, span_ref, sem, sums):
+    def through(make):
+        def span(step, carry):
+            local = t_ref[at.sequence + offset + step]
+            make(step, local, rows_of(q_ref, local))
+            worst_ref[...] = jnp.maximum(worst_ref[...], acc_ref[HD : HD + 8])
+            if len(o_refs) == 1:
+                conclude(acc_ref, rows_of(o_refs[0], local))
+                return carry
+            for index, o_ref in enumerate(o_refs):
+
+                @pl.when(step == index)
+                def _(o_ref=o_ref):
+                    conclude(acc_ref, o_ref)
+
+            return carry
+
+        lax.fori_loop(0, count, span, 0)
+
+    worst_ref[...] = jnp.zeros_like(worst_ref)
+    through(sums)
+
+    @pl.when(jnp.logical_not(jnp.max(worst_ref[...]) < 1e30))
     def _():
-        run_ref[...] = jnp.full_like(run_ref, -1e30)
-        acc_ref[...] = jnp.zeros_like(acc_ref)
-        for index, piece in enumerate(pieces):
-            base = t_ref[at.bases + index]
-
-            def careful(j, carry, piece=piece, base=base):
-                other = t_ref[at.order + base + j]
-
-                @pl.when(other <= p)
-                def _():
-                    copy = pltpu.make_async_copy(piece.at[j], span_ref, sem)
-                    copy.start()
-                    copy.wait()
-                    s = scores(span_ref[:SPAN], q_ref)
-                    s = jnp.where(other < p, s, causal(s))
-                    old = run_ref[...]
-                    new = jnp.maximum(old, jnp.max(s, axis=0, keepdims=True))
-                    run_ref[...] = new
-                    fresh = blend(span_ref[SPAN:], jnp.exp2(s - new[:1]))
-                    acc_ref[...] = acc_ref[...] * jnp.exp2(old - new)[:1] + fresh
-
-                return carry
-
-            lax.fori_loop(0, piece.shape[0], careful, 0)
+        def make(step, local, query):
+            p = t_ref[at.order + t_ref[at.first] + local]
+            careful(at, t_ref, p, query, pieces, acc_ref, run_ref, span_ref, sem)
+
+        through(make)
 
 
 def conclude(acc_ref, o_ref):
@@ -169,14 +198,11 @@
     t_ref, q_ref, acc_in, m_in = refs[:4]
     pieces = refs[4 : 4 + n_kv]
     o_refs = refs[4 + n_kv : 4 + n_kv + n_out]
-    acc_ref, run_ref, kv_ref, span_ref, sems = refs[4 + n_kv + n_out :]
+    kv_ref, acc_ref, worst_ref, run_ref, span_ref, sems = refs[4 + n_kv + n_out :]
     fetch(pieces[-1:], [kv_ref], sems)
 
-    def span(step, carry):
-        local = t_ref[at.sequence + offset + step]
-        stored = t_ref[at.first] + local
-        query = rows_of(q_ref, local)
-        count = t_ref[at.far_rank + stored]
+    def sums(step, local, query):
+        count = t_ref[at.far_rank + t_ref[at.first] + local]
 
         @pl.when(count == 0)
         def _():
@@ -191,43 +217,25 @@
                 weights = jnp.exp2(scores(keys, query) - m_in[skip + step, :1])
                 acc_ref[...] = acc_in[skip + step] + blend(values, weights)
 
-        recheck(at, t_ref, t_ref[at.order + stored], query, pieces, acc_ref, run_ref, span_ref, sems.at[0])
-        for index, o_ref in enumerate(o_refs):
-
-            @pl.when(step == index)
-            def _(o_ref=o_ref):
-                conclude(acc_ref, o_ref)
-
-        return carry
-
-    lax.fori_loop(0, n_out, span, 0)
+    each_span(
+        at, offset, n_out, t_ref, q_ref, pieces, o_refs, acc_ref, worst_ref, run_ref, span_ref, sems.at[0], sums
+    )
 
 
 def whole_kernel(at, offset, n_kv, count, *refs):
     t_ref, q_ref = refs[:2]
     pieces = refs[2 : 2 + n_kv]
-    o_refs = refs[2 + n_kv : -6]
-    acc_ref, m_ref, run_ref, kv_ref, span_ref, sems = refs[-6:]
+    o_refs = refs[2 + n_kv : -7]
+    m_ref, kv_ref, acc_ref, worst_ref, run_ref, span_ref, sems = refs[-7:]
     fetch(pieces, places(at, t_ref, kv_ref, pieces), sems)
 
-    def span(step, carry):
-        local = t_ref[at.sequence + offset + step]
+    def sums(step, local, query):
         p = t_ref[at.order + t_ref[at.first] + local]
-        query = rows_of(q_ref, local)
         attend(t_ref, at.all_list, p, query, kv_ref, acc_ref, m_ref)
-        recheck(at, t_ref, p, query, pieces, acc_ref, run_ref, span_ref, sems.at[0])
-        if len(o_refs) == 1:
-            conclude(acc_ref, rows_of(o_refs[0], local))
-        else:
-            for index, o_ref in enumerate(o_refs):
-
-                @pl.when(step == index)
-                def _(o_ref=o_ref):
-                    conclude(acc_ref, o_ref)
-
-        return carry
-
-    lax.fori_loop(0, count, span, 0)
+
+    each_span(
+        at, offset, count, t_ref, q_ref, pieces, o_refs, acc_ref, worst_ref, run_ref, span_ref, sems.at[0], sums
+    )
 
 
 def attention(q, near, far, near_bases, far_bases, far_first, first_span, span_order, sequence):
@@ -280,7 +288,7 @@
     def finish(begun, begun_at, offset, count):
         shapes = [jax.ShapeDtypeStruct((SPAN, GROUP * HD), q.dtype)] * count
         kernel = functools.partial(far_kernel, at, offset, offset - begun_at, n_kv, count)
-        scratch = [acc_like, m_like, pltpu.VMEM(far[0].shape, jnp.bfloat16), span_like]
+        scratch = [pltpu.VMEM(far[0].shape, jnp.bfloat16), acc_like, m_like, m_like, span_like]
         return call(kernel, "far", (table, q, *begun), near + far, shapes, scratch, 0.25 * count / q_spans)
 
     def whole(offset, count, q, apart):
@@ -289,7 +297,7 @@
         else:
             shapes = [jax.ShapeDtypeStruct(q.shape, q.dtype)]
         kernel = functools.partial(whole_kernel, at, offset, n_kv, count)
-        scratch = [acc_like, m_like, m_like, kv_like, span_like]
+        scratch = [m_like, kv_like, acc_like, m_like, m_like, span_like]
         return call(kernel, "whole", (table, q), near + far, shapes, scratch, count / q_spans)
 
     return begin, finish, whole

time: 93.6 us -> 93.1 us (level); the launches traced: 94.7 us -> 92.8 us
    ppermute x7, waiting for transfers between devices: 2.2 us -> 1.26 us  [send(): done = lax.ppermute(done, GROUP_AXES, [(i, i ^ step) for i in range(KVH)])]
  transfers between devices with their start and end apart: 12 -> 12, of which waited for: 6 -> 5; matrix products, arithmetic and copies ran while one was open for 2% -> 2% of each run, Pallas kernels for 31% -> 31%
where the time goes in v2:
time: 93.1 us; the launch traced here: 92.8 us
  Pallas kernels  35.6 us (38%)
  waiting for transfers between devices  31.3 us (34%)
  starting transfers between devices  23.4 us (25%)
  local copies, waits for them, and re-layouts  1.75 us (2%)
    pallas_call x4, Pallas kernels, call(): pl.pallas_call(kernel, in_specs=[smem] + [vmem] * (len(operands) - 1 + le...  32.1 us
    ppermute x1, waiting for transfers between devices, shards(): lax.ppermute(own, 'outer', [(i, (i + 1) % outer) for i in range(outer)])  12.1 us
    ppermute x7, starting transfers between devices, send(): done = lax.ppermute(done, GROUP_AXES, [(i, i ^ step) for i in range(KVH)])  10.6 us
    ppermute x1, waiting for transfers between devices, shards(): lax.ppermute(own, 'outer', [(i, (i - 1) % outer) for i in range(outer)])  10.2 us
    all_to_all x1, waiting for transfers between devices, to_head_owners(): return exchange(packed)  7.7 us
    all_to_all x1, starting transfers between devices, to_head_owners(): return exchange(packed)  5.17 us
    all_to_all x1, starting transfers between devices, shards(): lax.all_to_all(q, GROUP_AXES, split_axis=0, concat_axis=0, tiled=False)  3.74 us
    ppermute x1, starting transfers between devices, shards(): lax.ppermute(own, 'outer', [(i, (i - 1) % outer) for i in range(outer)])  2.25 us
  transfers between devices with their start and end apart: 12, of which 5 were waited for; matrix products, arithmetic and copies ran while one was open for 2% of the time, Pallas kernels for 31%

profile of v2, /device:TPU:0, one launch (start us, length us, event | category | flops | bytes accessed | tf_op | source)
XLA Modules:
  0.0 92.8 jit_solution(12510159162012470607)
XLA Ops:
  0.0 0.0 copy-start
  0.0 2.1 %pack.1 = bf16[8,256,128]{2,1,0:T(8,128)(2,1)} custom-call(bf16[128,1024]{1,0:T(8,128)(2,1)} %k_ref.1, bf16[128,1024]{1,0:T(8,128)(2,1)} %v_ref.1), custom_call_target="tpu_custom_call" | custom-call | tf_op jit(solution)/shard_map/pack/pallas_call | solution.py:358
  2.1 5.2 %all-to-all-start.1 = ((bf16[8,256,128]{2,1,0:T(8,128)(2,1)}), bf16[8,256,128]{2,1,0:T(8,128)(2,1)S(1)}, u32[]{:S(2)}, u32[]{:S(2)}) async-start(bf16[8,256,128]{2,1,0:T(8,128)(2,1)} %pack.1), calls=%async_computation.1 | async-start | bytes 1048576 | tf_op jit(solution)/shard_map/all_to_all | solution.py:361
  7.3 0.0 copy-done
  7.3 1.6 %copy.9 = bf16[16,8,8,1024]{3,2,0,1:T(8,128)(2,1)} copy(bf16[16,8,8,1024]{3,2,1,0:T(8,128)(2,1)S(1)} %bitcast.26) | data formatting | bytes 4194304 | tf_op jit(solution)/shard_map/reshape | solution.py:373
  8.8 7.7 %all-to-all-done.1.refs_2_.refs_4_ = bf16[8,256,128]{2,1,0:T(8,128)(2,1)S(1)} async-done(((bf16[8,256,128]{2,1,0:T(8,128)(2,1)}), bf16[8,256,128]{2,1,0:T(8,128)(2,1)S(1)}, u32[]{:S(2)}, u32[]{:S(2)}) %all-to-all-start.1) | async-done | bytes 524320 | tf_op jit(solution)/shard_map/all_to_all | solution.py:361
  16.5 0.0 copy-start.1
  16.5 3.7 %all-to-all-start = ((bf16[8,128,1024]{2,1,0:T(8,128)(2,1)}), bf16[8,128,1024]{2,1,0:T(8,128)(2,1)S(1)}, u32[]{:S(2)}, u32[]{:S(2)}) async-start(bf16[8,128,1024]{2,1,0:T(8,128)(2,1)} %bitcast.25), calls=%async_computation | async-start | bytes 4194304 | tf_op jit(solution)/shard_map/all_to_all | solution.py:374
  20.3 1.6 %collective-permute-start = (bf16[8,256,128]{2,1,0:T(8,128)(2,1)S(1)}, bf16[8,256,128]{2,1,0:T(8,128)(2,1)S(1)}, u32[]{:S(2)}, u32[]{:S(2)}) collective-permute-start(bf16[8,256,128]{2,1,0:T(8,128)(2,1)S(1)} %all-to-all-done.1.refs_2_.refs_4_), channel_id=1, source_target_pairs={{0,8},{8,16},{16,24},{24,0},{1,9},{9,17},{17,25},{25,1},{2,10},{10... | collective-permute-start | bytes 1572872 | tf_op jit(solution)/shard_map/ppermute | solution.py:376
  21.9 2.2 %collective-permute-start.1 = (bf16[8,256,128]{2,1,0:T(8,128)(2,1)S(1)}, bf16[8,256,128]{2,1,0:T(8,128)(2,1)}, u32[]{:S(2)}, u32[]{:S(2)}) collective-permute-start(bf16[8,256,128]{2,1,0:T(8,128)(2,1)S(1)} %all-to-all-done.1.refs_2_.refs_4_), channel_id=1, source_target_pairs={{0,24},{8,0},{16,8},{24,16},{1,25},{9,1},{17,9},{25,17},{2,26},{10... | collective-permute-start | bytes 1572872 | tf_op jit(solution)/shard_map/ppermute | solution.py:377
  24.2 0.1 stack.46
  24.3 0.0 copy-done.1
  24.3 0.2 fusion
  24.5 0.1 select_reduce_fusion
  24.6 0.1 select_reduce_fusion.1
  24.7 0.1 concatenate.3.refs_0_
  24.8 12.1 %collective-permute-done.refs_3_.refs_5_ = bf16[8,256,128]{2,1,0:T(8,128)(2,1)S(1)} collective-permute-done((bf16[8,256,128]{2,1,0:T(8,128)(2,1)S(1)}, bf16[8,256,128]{2,1,0:T(8,128)(2,1)S(1)}, u32[]{:S(2)}, u32[]{:S(2)}) %collective-permute-start) | collective-permute-done | bytes 524320 | tf_op jit(solution)/shard_map/ppermute | solution.py:376
  36.9 0.0 collective-permute-start.2
  36.9 10.2 %collective-permute-done.1.refs_4_.refs_6_ = bf16[8,256,128]{2,1,0:T(8,128)(2,1)} collective-permute-done((bf16[8,256,128]{2,1,0:T(8,128)(2,1)S(1)}, bf16[8,256,128]{2,1,0:T(8,128)(2,1)}, u32[]{:S(2)}, u32[]{:S(2)}) %collective-permute-start.1) | collective-permute-done | bytes 524320 | tf_op jit(solution)/shard_map/ppermute | solution.py:377
  47.2 0.0 all-to-all-done
  47.2 13.1 %near.1 = (f32[6,144,1024]{2,1,0:T(8,128)S(1)}, f32[6,8,1024]{2,1,0:T(8,128)S(1)}) custom-call(s32[216]{0:T(256)S(1)} %concatenate.3.refs_0_, bf16[1024,1024]{1,0:T(8,128)(2,1)S(1)} %bitcast.21, bf16[8,256,128]{2,1,0:T(8,128)(2,1)S(1)} %all-to-all-done.1.refs_2_.refs_4_, bf16[8,256,128]{2,1,0:T(8,128)(2,1)S(1)} %collective-permute-done.refs_3_.refs_5_, ...), custom_call_target="tpu_custom_call" | custom-call | flops 9663676416 | bytes 4456448 | tf_op jit(solution)/shard_map/near/pallas_call | solution.py:265
  60.2 0.0 collective-permute-done.2.refs_7_.refs_5_
  60.3 3.8 %far.3 = (bf16[128,1024]{1,0:T(8,128)(2,1)S(1)}, bf16[128,1024]{1,0:T(8,128)(2,1)S(1)}) custom-call(s32[216]{0:T(256)S(1)} %concatenate.3.refs_0_, bf16[1024,1024]{1,0:T(8,128)(2,1)S(1)} %bitcast.22, f32[6,144,1024]{2,1,0:T(8,128)S(1)} %get-tuple-element.16.refs_2_, f32[6,8,1024]{2,1,0:T(8,128)S(1)} %get-tuple-element.17.refs_3_, ...), custom_call_target="tpu_custom_call" | custom-call | flops 1073741824 | bytes 2359296 | tf_op jit(solution)/shard_map/far/pallas_call | solution.py:265
  64.0 3.6 %collective-permute-start.3 = (bf16[128,1024]{1,0:T(8,128)(2,1)S(1)}, bf16[128,1024]{1,0:T(8,128)(2,1)S(1)}, u32[]{:S(2)}, u32[]{:S(2)}) collective-permute-start(bf16[128,1024]{1,0:T(8,128)(2,1)S(1)} %get-tuple-element.22), channel_id=1, source_target_pairs={{0,5},{1,4},{2,7},{3,6},{4,1},{5,0},{6,3},{7,2},{8,13},{9,12},{10,... | collective-permute-start | bytes 786440 | tf_op jit(solution)/shard_map/ppermute | solution.py:324
  67.6 0.0 collective-permute-start.4
  67.6 5.7 %far.2 = (bf16[128,1024]{1,0:T(8,128)(2,1)S(1)}, bf16[128,1024]{1,0:T(8,128)(2,1)S(1)}, bf16[128,1024]{1,0:T(8,128)(2,1)S(1)}, bf16[128,1024]{1,0:T(8,128)(2,1)S(1)}) custom-call(s32[216]{0:T(256)S(1)} %concatenate.3.refs_0_, bf16[1024,1024]{1,0:T(8,128)(2,1)S(1)} %bitcast.23, f32[6,144,1024]{2,1,0:T(8,128)S(1)} %get-tuple-element.16.refs_2_, ...), custom_call_target="tpu_custom_call" | custom-call | flops 2147483648 | bytes 2621440 | tf_op jit(solution)/shard_map/far/pallas_call | solution.py:265
  73.4 3.6 %collective-permute-start.5 = (bf16[128,1024]{1,0:T(8,128)(2,1)S(1)}, bf16[128,1024]{1,0:T(8,128)(2,1)S(1)}, u32[]{:S(2)}, u32[]{:S(2)}) collective-permute-start(bf16[128,1024]{1,0:T(8,128)(2,1)S(1)} %get-tuple-element.18), channel_id=1, source_target_pairs={{0,1},{1,0},{2,3},{3,2},{4,5},{5,4},{6,7},{7,6},{8,9},{9,8},{10,11... | collective-permute-start | bytes 786440 | tf_op jit(solution)/shard_map/ppermute | solution.py:324
  77.0 1.1 %collective-permute-start.7 = (bf16[128,1024]{1,0:T(8,128)(2,1)S(1)}, bf16[128,1024]{1,0:T(8,128)(2,1)S(1)}, u32[]{:S(2)}, u32[]{:S(2)}) collective-permute-start(bf16[128,1024]{1,0:T(8,128)(2,1)S(1)} %get-tuple-element.20), channel_id=1, source_target_pairs={{0,3},{1,2},{2,1},{3,0},{4,7},{5,6},{6,5},{7,4},{8,11},{9,10},{10,... | collective-permute-start | bytes 786440 | tf_op jit(solution)/shard_map/ppermute | solution.py:324
  78.2 0.3 collective-permute-start.8
  78.4 0.0 collective-permute-done.3.refs_5_
  78.4 1.1 %collective-permute-start.9 = (bf16[128,1024]{1,0:T(8,128)(2,1)S(1)}, bf16[128,1024]{1,0:T(8,128)(2,1)S(1)}, u32[]{:S(2)}, u32[]{:S(2)}) collective-permute-start(bf16[128,1024]{1,0:T(8,128)(2,1)S(1)} %get-tuple-element.21), channel_id=1, source_target_pairs={{0,6},{1,7},{2,4},{3,5},{4,2},{5,3},{6,0},{7,1},{8,14},{9,15},{10,... | collective-permute-start | bytes 786440 | tf_op jit(solution)/shard_map/ppermute | solution.py:324
  79.5 0.0 collective-permute-done.4.refs_7_
  79.6 9.6 %whole.1 = (bf16[128,1024]{1,0:T(8,128)(2,1)S(1)}, bf16[128,1024]{1,0:T(8,128)(2,1)S(1)}) custom-call(s32[216]{0:T(256)S(1)} %concatenate.3.refs_0_, bf16[1024,1024]{1,0:T(8,128)(2,1)S(1)} %bitcast.24, bf16[8,256,128]{2,1,0:T(8,128)(2,1)S(1)} %all-to-all-done.1.refs_2_.refs_4_, bf16[8,256,128]{2,1,0:T(8,128)(2,1)S(1)} %collective-permute-done.refs_3_.refs_5_, ...), custom_call_target="tpu_custom_call" | custom-call | flops 4294967296 | bytes 3145728 | tf_op jit(solution)/shard_map/whole/pallas_call | solution.py:265
  89.1 0.8 collective-permute-start.6
  89.9 0.0 collective-permute-done.5.refs_1_
  90.0 0.7 collective-permute-done.7.refs_3_
  90.6 0.0 collective-permute-done.8.refs_4_
  90.6 0.6 collective-permute-done.9.refs_6_
  91.2 0.0 collective-permute-done.6.refs_2_
  91.2 1.4 %unpack.1 = bf16[128,8192]{1,0:T(8,128)(2,1)} custom-call(s32[1]{0:T(128)} %bitcast.me_ref, bf16[128,1024]{1,0:T(8,128)(2,1)S(1)} %get-tuple-element.25.refs_0_, bf16[128,1024]{1,0:T(8,128)(2,1)S(1)} %collective-permute-done.5.refs_1_, bf16[128,1024]{1,0:T(8,128)(2,1)S(1)} %collective-permute-done.6.refs_2_, ...), custom_call_target="tpu_custom_call" | custom-call | tf_op jit(solution)/shard_map/unpack/pallas_call | solution.py:335
  (2 shorter events, 0.0 us)
Async XLA Ops:
  0.0 7.3 %copy-start = (bf16[128,8192]{1,0:T(8,128)(2,1)S(1)}, bf16[128,8192]{1,0:T(8,128)(2,1)}, u32[]{:S(2)}) copy-start(bf16[128,8192]{1,0:T(8,128)(2,1)} %param.4) | copy-start | bytes 6291460
  2.1 14.4 %all-to-all-start.1 = ((bf16[8,256,128]{2,1,0:T(8,128)(2,1)}), bf16[8,256,128]{2,1,0:T(8,128)(2,1)S(1)}, u32[]{:S(2)}, u32[]{:S(2)}) async-start(bf16[8,256,128]{2,1,0:T(8,128)(2,1)} %pack.1), calls=%async_computation.1 | async-start | bytes 1048576 | tf_op jit(solution)/shard_map/all_to_all | solution.py:361
  16.5 7.7 %copy-start.1 = (s32[32]{0:T(128)S(1)}, s32[32]{0:T(128)}, u32[]{:S(2)}) copy-start(s32[32]{0:T(128)} %param.7) | copy-start | bytes 388
  16.5 30.6 %all-to-all-start = ((bf16[8,128,1024]{2,1,0:T(8,128)(2,1)}), bf16[8,128,1024]{2,1,0:T(8,128)(2,1)S(1)}, u32[]{:S(2)}, u32[]{:S(2)}) async-start(bf16[8,128,1024]{2,1,0:T(8,128)(2,1)} %bitcast.25), calls=%async_computation | async-start | bytes 4194304 | tf_op jit(solution)/shard_map/all_to_all | solution.py:374
  20.3 16.6 %collective-permute-start = (bf16[8,256,128]{2,1,0:T(8,128)(2,1)S(1)}, bf16[8,256,128]{2,1,0:T(8,128)(2,1)S(1)}, u32[]{:S(2)}, u32[]{:S(2)}) collective-permute-start(bf16[8,256,128]{2,1,0:T(8,128)(2,1)S(1)} %all-to-all-done.1.refs_2_.refs_4_), channel_id=1, source_target_pairs={{0,8},{8,16},{16,24},{24,0},{1,9},{9,17},{17,25},{25,1},{2,10},{10... | collective-permute-start | bytes 1572872 | tf_op jit(solution)/shard_map/ppermute | solution.py:376
  21.9 25.2 %collective-permute-start.1 = (bf16[8,256,128]{2,1,0:T(8,128)(2,1)S(1)}, bf16[8,256,128]{2,1,0:T(8,128)(2,1)}, u32[]{:S(2)}, u32[]{:S(2)}) collective-permute-start(bf16[8,256,128]{2,1,0:T(8,128)(2,1)S(1)} %all-to-all-done.1.refs_2_.refs_4_), channel_id=1, source_target_pairs={{0,24},{8,0},{16,8},{24,16},{1,25},{9,1},{17,9},{25,17},{2,26},{10... | collective-permute-start | bytes 1572872 | tf_op jit(solution)/shard_map/ppermute | solution.py:377
  36.9 23.3 %collective-permute-start.2 = (bf16[8,256,128]{2,1,0:T(8,128)(2,1)S(1)}, bf16[8,256,128]{2,1,0:T(8,128)(2,1)}, u32[]{:S(2)}, u32[]{:S(2)}) collective-permute-start(bf16[8,256,128]{2,1,0:T(8,128)(2,1)S(1)} %collective-permute-done.refs_3_.refs_5_), channel_id=1, source_target_pairs={{0,8},{8,16},{16,24},{24,0},{1,9},{9,17},{17,25},{25,1},{2,10},{10... | collective-permute-start | bytes 1572872 | tf_op jit(solution)/shard_map/ppermute | solution.py:378
  64.0 14.4 %collective-permute-start.3 = (bf16[128,1024]{1,0:T(8,128)(2,1)S(1)}, bf16[128,1024]{1,0:T(8,128)(2,1)S(1)}, u32[]{:S(2)}, u32[]{:S(2)}) collective-permute-start(bf16[128,1024]{1,0:T(8,128)(2,1)S(1)} %get-tuple-element.22), channel_id=1, source_target_pairs={{0,5},{1,4},{2,7},{3,6},{4,1},{5,0},{6,3},{7,2},{8,13},{9,12},{10,... | collective-permute-start | bytes 786440 | tf_op jit(solution)/shard_map/ppermute | solution.py:324
  67.6 11.9 %collective-permute-start.4 = (bf16[128,1024]{1,0:T(8,128)(2,1)S(1)}, bf16[128,1024]{1,0:T(8,128)(2,1)S(1)}, u32[]{:S(2)}, u32[]{:S(2)}) collective-permute-start(bf16[128,1024]{1,0:T(8,128)(2,1)S(1)} %get-tuple-element.23), channel_id=1, source_target_pairs={{0,7},{1,6},{2,5},{3,4},{4,3},{5,2},{6,1},{7,0},{8,15},{9,14},{10,... | collective-permute-start | bytes 786440 | tf_op jit(solution)/shard_map/ppermute | solution.py:324
  73.4 16.6 %collective-permute-start.5 = (bf16[128,1024]{1,0:T(8,128)(2,1)S(1)}, bf16[128,1024]{1,0:T(8,128)(2,1)S(1)}, u32[]{:S(2)}, u32[]{:S(2)}) collective-permute-start(bf16[128,1024]{1,0:T(8,128)(2,1)S(1)} %get-tuple-element.18), channel_id=1, source_target_pairs={{0,1},{1,0},{2,3},{3,2},{4,5},{5,4},{6,7},{7,6},{8,9},{9,8},{10,11... | collective-permute-start | bytes 786440 | tf_op jit(solution)/shard_map/ppermute | solution.py:324
  77.0 13.6 %collective-permute-start.7 = (bf16[128,1024]{1,0:T(8,128)(2,1)S(1)}, bf16[128,1024]{1,0:T(8,128)(2,1)S(1)}, u32[]{:S(2)}, u32[]{:S(2)}) collective-permute-start(bf16[128,1024]{1,0:T(8,128)(2,1)S(1)} %get-tuple-element.20), channel_id=1, source_target_pairs={{0,3},{1,2},{2,1},{3,0},{4,7},{5,6},{6,5},{7,4},{8,11},{9,10},{10,... | collective-permute-start | bytes 786440 | tf_op jit(solution)/shard_map/ppermute | solution.py:324
  78.2 12.5 %collective-permute-start.8 = (bf16[128,1024]{1,0:T(8,128)(2,1)S(1)}, bf16[128,1024]{1,0:T(8,128)(2,1)S(1)}, u32[]{:S(2)}, u32[]{:S(2)}) collective-permute-start(bf16[128,1024]{1,0:T(8,128)(2,1)S(1)} %get-tuple-element.19), channel_id=1, source_target_pairs={{0,4},{1,5},{2,6},{3,7},{4,0},{5,1},{6,2},{7,3},{8,12},{9,13},{10,... | collective-permute-start | bytes 786440 | tf_op jit(solution)/shard_map/ppermute | solution.py:324
  78.4 12.8 %collective-permute-start.9 = (bf16[128,1024]{1,0:T(8,128)(2,1)S(1)}, bf16[128,1024]{1,0:T(8,128)(2,1)S(1)}, u32[]{:S(2)}, u32[]{:S(2)}) collective-permute-start(bf16[128,1024]{1,0:T(8,128)(2,1)S(1)} %get-tuple-element.21), channel_id=1, source_target_pairs={{0,6},{1,7},{2,4},{3,5},{4,2},{5,3},{6,0},{7,1},{8,14},{9,15},{10,... | collective-permute-start | bytes 786440 | tf_op jit(solution)/shard_map/ppermute | solution.py:324
  89.1 2.1 %collective-permute-start.6 = (bf16[128,1024]{1,0:T(8,128)(2,1)S(1)}, bf16[128,1024]{1,0:T(8,128)(2,1)S(1)}, u32[]{:S(2)}, u32[]{:S(2)}) collective-permute-start(bf16[128,1024]{1,0:T(8,128)(2,1)S(1)} %get-tuple-element.26), channel_id=1, source_target_pairs={{0,2},{1,3},{2,0},{3,1},{4,6},{5,7},{6,4},{7,5},{8,10},{9,11},{10,... | collective-permute-start | bytes 786440 | tf_op jit(solution)/shard_map/ppermute | solution.py:324
